TPU v7x, 32 devices: a whole 2x2x4 slice. The times are simulated.
32 devices in a mesh: dp: 32 (over z, y, x, core).
Axes of the slice: x: 2, y: 2, z: 4, core: 2. Of those that a mesh axis runs over, the one named last changes fastest.
Arguments:
- tokens: bfloat16 [49152, 768], P('dp'), may hold values from -6 to 6
- buckets: int32 [128], P('dp'), may hold values from 0 to 2, as said below
- lengths: int32 [128], P('dp'), may hold values from 88 to 384, as said below
- w_query: bfloat16 [768, 768], P('dp'), may hold values from -0.21875 to 0.21875
- w_key: bfloat16 [768, 768], P('dp'), may hold values from -0.21875 to 0.21875
- w_value: bfloat16 [768, 768], P('dp'), may hold values from -0.21875 to 0.21875
- w_output: bfloat16 [768, 768], P('dp'), may hold values from -2 to 2
- bias_query: bfloat16 [768], P('dp'), may hold values from -3 to 3
- bias_value: bfloat16 [768], P('dp'), may hold values from -3 to 3
- bias_output: bfloat16 [768], P('dp'), may hold values from -3 to 3
- gain_first: bfloat16 [768], P('dp'), may hold values from 0.5 to 1.5
- shift_first: bfloat16 [768], P('dp'), may hold values from -2 to 2
- w_expand: bfloat16 [768, 3072], P('dp'), may hold values from -0.21875 to 0.21875
- bias_expand: bfloat16 [3072], P('dp'), may hold values from -3 to 3
- w_shrink: bfloat16 [3072, 768], P('dp'), may hold values from -0.15625 to 0.15625
- bias_shrink: bfloat16 [768], P('dp'), may hold values from -3 to 3
- gain_second: bfloat16 [768], P('dp'), may hold values from 0.5 to 1.5
- shift_second: bfloat16 [768], P('dp'), may hold values from -2 to 2
- grad_out: bfloat16 [49152, 768], P('dp'), may hold values from -6 to 6
Outputs:
- layer_out: bfloat16 [49152, 768], P('dp')
- grad_tokens: float32 [49152, 768], P('dp')
- grad_w_query: float32 [768, 768], P('dp')
- grad_w_key: float32 [768, 768], P('dp')
- grad_w_value: float32 [768, 768], P('dp')
- grad_w_output: float32 [768, 768], P('dp')
- grad_bias_query: float32 [768], P('dp')
- grad_bias_value: float32 [768], P('dp')
- grad_bias_output: float32 [768], P('dp')
- grad_gain_first: float32 [768], P('dp')
- grad_shift_first: float32 [768], P('dp')
- grad_w_expand: float32 [768, 3072], P('dp')
- grad_bias_expand: float32 [3072], P('dp')
- grad_w_shrink: float32 [3072, 768], P('dp')
- grad_bias_shrink: float32 [768], P('dp')
- grad_gain_second: float32 [768], P('dp')
- grad_shift_second: float32 [768], P('dp')
Inputs may be any that keep to these rules, and one draw needn't show every extreme that they name: `buckets`: bucket of each sequence: 0, 1 or 2 for 176, 224 or 384 rows; a sequence fills the first rows of its slot of 384 rows. `lengths`: true length of each sequence: at least half of its bucket's rows (rounded down), at most all of them; keys at or past it are padding.
All inputs are finite; a program needn't handle non-finite values.
Results may differ from a plain program's by a relative error of at most 0.014.
The roundings to bfloat16 on the way count: a program that leaves them out, or rounds other values in their place, can miss the bound.
Values may be sent and summed in bfloat16 or wider, within the bound.
No kernel may reach another device: no remote copies, remote signals or barrier semaphores. Data moves between devices by JAX's collectives and lax.ppermute only.
A program may use at most 256 MiB of HBM per device.

v0:
```python
import math

import jax
import jax.numpy as jnp
from jax import lax
from jax.sharding import PartitionSpec as P

D = 768
H = 12
HD = 64
B0 = 176
B1 = 224
B2 = 384


epsilon = 1e-12


def norm_parts(hidden):
    row_mean = jnp.mean(hidden, -1, keepdims=True)
    centred = hidden - row_mean
    inverse_root = lax.rsqrt(jnp.mean(centred * centred, -1, keepdims=True) + epsilon)
    return (centred * inverse_root, inverse_root)


def norm_back(upstream, normed, inverse_root, gain_vec):
    scaled = upstream * gain_vec
    return inverse_root * (
        scaled
        - jnp.mean(scaled, -1, keepdims=True)
        - normed * jnp.mean(scaled * normed, -1, keepdims=True)
    )


def attention_forward(tokens, attn_params, key_mask, slot_count):
    (
        full_query,
        full_key,
        full_value,
        full_output,
        full_bias_query,
        full_bias_value,
        full_bias_output,
        full_gain,
        full_shift,
    ) = attn_params
    row_count = tokens.shape[0]
    length = row_count // slot_count
    score_scale = 1.0 / math.sqrt(HD)
    queries = (
        (
            jnp.dot(tokens, full_query, preferred_element_type=jnp.float32)
            + full_bias_query.astype(jnp.float32)
        )
        .astype(jnp.bfloat16)
        .reshape(slot_count, length, H, HD)
    )
    key_rows = jnp.dot(tokens, full_key, preferred_element_type=jnp.float32).astype(jnp.bfloat16)
    key_rows = key_rows.reshape(slot_count, length, H, HD)
    value_rows = (
        (
            jnp.dot(tokens, full_value, preferred_element_type=jnp.float32)
            + full_bias_value.astype(jnp.float32)
        )
        .astype(jnp.bfloat16)
        .reshape(slot_count, length, H, HD)
    )
    scores = (
        jnp.einsum("sihe,sjhe->shij", queries, key_rows, preferred_element_type=jnp.float32)
        * score_scale
    )
    scores = jnp.where(key_mask[:, None, None, :], scores, -1e30)
    row_peak = jnp.max(scores, -1, keepdims=True)
    exp_terms = jnp.exp(scores - row_peak)
    soft_full = exp_terms / jnp.sum(exp_terms, -1, keepdims=True)
    soft_low = soft_full.astype(jnp.bfloat16)
    context = jnp.einsum(
        "shij,sjhe->sihe", soft_low, value_rows, preferred_element_type=jnp.float32
    )
    context = context.reshape(row_count, D).astype(jnp.bfloat16)
    attended = jnp.dot(
        context, full_output, preferred_element_type=jnp.float32
    ) + full_bias_output.astype(jnp.float32)
    normed, inverse_root = norm_parts(tokens.astype(jnp.float32) + attended)
    first = normed * full_gain.astype(jnp.float32) + full_shift.astype(jnp.float32)
    return (
        first,
        (queries, key_rows, value_rows, soft_full, soft_low, context, normed, inverse_root),
    )


def ffn_forward(first, ffn_params, row_mask):
    full_expand, full_bias_expand, full_shrink, full_bias_shrink, full_gain, full_shift = ffn_params
    first_low = first.astype(jnp.bfloat16)
    expand = jnp.dot(
        first_low, full_expand, preferred_element_type=jnp.float32
    ) + full_bias_expand.astype(jnp.float32)
    active = jax.nn.gelu(expand, approximate=False).astype(jnp.bfloat16)
    shrink = jnp.dot(
        active, full_shrink, preferred_element_type=jnp.float32
    ) + full_bias_shrink.astype(jnp.float32)
    normed, inverse_root = norm_parts(first + shrink)
    output = (normed * full_gain.astype(jnp.float32) + full_shift.astype(jnp.float32)) * row_mask[
        :, None
    ]
    return (output, (first_low, expand, active, normed, inverse_root))


def body(
    tokens,
    buckets,
    lengths,
    w_query,
    w_key,
    w_value,
    w_output,
    bias_query,
    bias_value,
    bias_output,
    gain_first,
    shift_first,
    w_expand,
    bias_expand,
    w_shrink,
    bias_shrink,
    gain_second,
    shift_second,
    grad_out,
):
    slot_count = buckets.shape[0]
    row_count = tokens.shape[0]
    length = row_count // slot_count
    score_scale = 1.0 / math.sqrt(HD)
    positions = jnp.arange(length, dtype=jnp.int32)
    bucket_rows = jnp.where(buckets == 0, B0, jnp.where(buckets == 1, B1, B2)).astype(jnp.int32)
    row_mask = (positions[None, :] < bucket_rows[:, None]).astype(jnp.float32).reshape(row_count)
    key_mask = positions[None, :] < lengths[:, None]
    attn_params = (
        lax.all_gather(w_query, "dp", axis=0, tiled=True),
        lax.all_gather(w_key, "dp", axis=0, tiled=True),
        lax.all_gather(w_value, "dp", axis=0, tiled=True),
        lax.all_gather(w_output, "dp", axis=0, tiled=True),
        lax.all_gather(bias_query, "dp", axis=0, tiled=True),
        lax.all_gather(bias_value, "dp", axis=0, tiled=True),
        lax.all_gather(bias_output, "dp", axis=0, tiled=True),
        lax.all_gather(gain_first, "dp", axis=0, tiled=True),
        lax.all_gather(shift_first, "dp", axis=0, tiled=True),
    )
    first, unused_attn = attention_forward(tokens, attn_params, key_mask, slot_count)
    ffn_params = (
        lax.all_gather(w_expand, "dp", axis=0, tiled=True),
        lax.all_gather(bias_expand, "dp", axis=0, tiled=True),
        lax.all_gather(w_shrink, "dp", axis=0, tiled=True),
        lax.all_gather(bias_shrink, "dp", axis=0, tiled=True),
        lax.all_gather(gain_second, "dp", axis=0, tiled=True),
        lax.all_gather(shift_second, "dp", axis=0, tiled=True),
    )
    output, unused_ffn = ffn_forward(first, ffn_params, row_mask)
    layer_out = output.astype(jnp.bfloat16)
    ffn_back = (
        lax.all_gather(w_expand, "dp", axis=0, tiled=True),
        lax.all_gather(bias_expand, "dp", axis=0, tiled=True),
        lax.all_gather(w_shrink, "dp", axis=0, tiled=True),
        lax.all_gather(bias_shrink, "dp", axis=0, tiled=True),
        lax.all_gather(gain_second, "dp", axis=0, tiled=True),
        lax.all_gather(shift_second, "dp", axis=0, tiled=True),
    )
    unused_out, (first_low, expand, active, normed_second, root_second) = ffn_forward(
        first, ffn_back, row_mask
    )
    (
        full_expand,
        full_bias_expand,
        full_shrink,
        full_bias_shrink,
        full_gain_second,
        full_shift_second,
    ) = ffn_back
    upstream = grad_out.astype(jnp.float32) * row_mask[:, None]
    grad_gain_second = jnp.sum(upstream * normed_second, 0)
    grad_shift_second = jnp.sum(upstream, 0)
    grad_second = norm_back(
        upstream, normed_second, root_second, full_gain_second.astype(jnp.float32)
    )
    grad_shrink_rows = grad_second.astype(jnp.bfloat16)
    grad_bias_shrink = jnp.sum(grad_shrink_rows.astype(jnp.float32), 0)
    grad_w_shrink = jnp.einsum(
        "rf,rd->fd", active, grad_shrink_rows, preferred_element_type=jnp.float32
    )
    grad_active = jnp.einsum(
        "rd,fd->rf", grad_shrink_rows, full_shrink, preferred_element_type=jnp.float32
    )
    unused_gelu, gelu_pull = jax.vjp(
        lambda pre_act: jax.nn.gelu(pre_act, approximate=False), expand
    )
    grad_expand_rows = gelu_pull(grad_active)[0].astype(jnp.bfloat16)
    grad_bias_expand = jnp.sum(grad_expand_rows.astype(jnp.float32), 0)
    grad_w_expand = jnp.einsum(
        "rd,rf->df", first_low, grad_expand_rows, preferred_element_type=jnp.float32
    )
    grad_first = grad_second + jnp.einsum(
        "rf,df->rd", grad_expand_rows, full_expand, preferred_element_type=jnp.float32
    )
    ffn_owned = (
        lax.psum_scatter(grad_w_expand, "dp", scatter_dimension=0, tiled=True),
        lax.psum_scatter(grad_bias_expand, "dp", scatter_dimension=0, tiled=True),
        lax.psum_scatter(grad_w_shrink, "dp", scatter_dimension=0, tiled=True),
        lax.psum_scatter(grad_bias_shrink, "dp", scatter_dimension=0, tiled=True),
        lax.psum_scatter(grad_gain_second, "dp", scatter_dimension=0, tiled=True),
        lax.psum_scatter(grad_shift_second, "dp", scatter_dimension=0, tiled=True),
    )
    attn_back = (
        lax.all_gather(w_query, "dp", axis=0, tiled=True),
        lax.all_gather(w_key, "dp", axis=0, tiled=True),
        lax.all_gather(w_value, "dp", axis=0, tiled=True),
        lax.all_gather(w_output, "dp", axis=0, tiled=True),
        lax.all_gather(bias_query, "dp", axis=0, tiled=True),
        lax.all_gather(bias_value, "dp", axis=0, tiled=True),
        lax.all_gather(bias_output, "dp", axis=0, tiled=True),
        lax.all_gather(gain_first, "dp", axis=0, tiled=True),
        lax.all_gather(shift_first, "dp", axis=0, tiled=True),
    )
    unused_first, saved = attention_forward(tokens, attn_back, key_mask, slot_count)
    queries, key_rows, value_rows, soft_full, soft_low, context, normed_first, root_first = saved
    (
        full_query,
        full_key,
        full_value,
        full_output,
        full_bias_query,
        full_bias_value,
        full_bias_output,
        full_gain_first,
        full_shift_first,
    ) = attn_back
    grad_gain_first = jnp.sum(grad_first * normed_first, 0)
    grad_shift_first = jnp.sum(grad_first, 0)
    grad_resid = norm_back(
        grad_first, normed_first, root_first, full_gain_first.astype(jnp.float32)
    )
    grad_attended = grad_resid.astype(jnp.bfloat16)
    grad_bias_output = jnp.sum(grad_attended.astype(jnp.float32), 0)
    grad_w_output = jnp.einsum(
        "rc,rd->cd", context, grad_attended, preferred_element_type=jnp.float32
    )
    grad_context = jnp.einsum(
        "rd,cd->rc", grad_attended, full_output, preferred_element_type=jnp.float32
    )
    grad_context = grad_context.astype(jnp.bfloat16).reshape(slot_count, length, H, HD)
    grad_soft = jnp.einsum(
        "sihe,sjhe->shij", grad_context, value_rows, preferred_element_type=jnp.float32
    )
    grad_values = jnp.einsum(
        "shij,sihe->sjhe", soft_low, grad_context, preferred_element_type=jnp.float32
    )
    grad_values = grad_values.astype(jnp.bfloat16).reshape(row_count, D)
    row_delta = jnp.sum(soft_full * grad_soft, -1, keepdims=True)
    grad_scores = (soft_full * (grad_soft - row_delta)).astype(jnp.bfloat16)
    grad_queries = jnp.einsum(
        "shij,sjhe->sihe", grad_scores, key_rows, preferred_element_type=jnp.float32
    )
    grad_queries = (grad_queries * score_scale).astype(jnp.bfloat16).reshape(row_count, D)
    grad_keys = jnp.einsum(
        "shij,sihe->sjhe", grad_scores, queries, preferred_element_type=jnp.float32
    )
    grad_keys = (grad_keys * score_scale).astype(jnp.bfloat16).reshape(row_count, D)
    grad_w_query = jnp.einsum("rc,rd->cd", tokens, grad_queries, preferred_element_type=jnp.float32)
    grad_w_key = jnp.einsum("rc,rd->cd", tokens, grad_keys, preferred_element_type=jnp.float32)
    grad_w_value = jnp.einsum("rc,rd->cd", tokens, grad_values, preferred_element_type=jnp.float32)
    grad_bias_query = jnp.sum(grad_queries.astype(jnp.float32), 0)
    grad_bias_value = jnp.sum(grad_values.astype(jnp.float32), 0)
    grad_tokens = (
        grad_resid
        + jnp.einsum("rd,cd->rc", grad_queries, full_query, preferred_element_type=jnp.float32)
        + jnp.einsum("rd,cd->rc", grad_keys, full_key, preferred_element_type=jnp.float32)
        + jnp.einsum("rd,cd->rc", grad_values, full_value, preferred_element_type=jnp.float32)
    )
    attn_owned = (
        lax.psum_scatter(grad_w_query, "dp", scatter_dimension=0, tiled=True),
        lax.psum_scatter(grad_w_key, "dp", scatter_dimension=0, tiled=True),
        lax.psum_scatter(grad_w_value, "dp", scatter_dimension=0, tiled=True),
        lax.psum_scatter(grad_w_output, "dp", scatter_dimension=0, tiled=True),
        lax.psum_scatter(grad_bias_query, "dp", scatter_dimension=0, tiled=True),
        lax.psum_scatter(grad_bias_value, "dp", scatter_dimension=0, tiled=True),
        lax.psum_scatter(grad_bias_output, "dp", scatter_dimension=0, tiled=True),
        lax.psum_scatter(grad_gain_first, "dp", scatter_dimension=0, tiled=True),
        lax.psum_scatter(grad_shift_first, "dp", scatter_dimension=0, tiled=True),
    )
    owned = tuple(attn_owned) + tuple(ffn_owned)
    return (
        layer_out,
        grad_tokens,
        owned[0],
        owned[1],
        owned[2],
        owned[3],
        owned[4],
        owned[5],
        owned[6],
        owned[7],
        owned[8],
        owned[9],
        owned[10],
        owned[11],
        owned[12],
        owned[13],
        owned[14],
    )


def solution(mesh):
    placed = (
        P("dp", None),
        P("dp"),
        P("dp"),
        P("dp", None),
        P("dp", None),
        P("dp", None),
        P("dp", None),
        P("dp"),
        P("dp"),
        P("dp"),
        P("dp"),
        P("dp"),
        P("dp", None),
        P("dp"),
        P("dp", None),
        P("dp"),
        P("dp"),
        P("dp"),
        P("dp", None),
    )
    return jax.shard_map(
        body,
        mesh=mesh,
        in_specs=placed,
        out_specs=(
            P("dp", None),
            P("dp", None),
            P("dp", None),
            P("dp", None),
            P("dp", None),
            P("dp", None),
            P("dp"),
            P("dp"),
            P("dp"),
            P("dp"),
            P("dp"),
            P("dp", None),
            P("dp"),
            P("dp", None),
            P("dp"),
            P("dp"),
            P("dp"),
        ),
        check_vma=False,
    )
```

profile of v0, /device:TPU:0, one launch (start us, length us, event | category | flops | bytes accessed | tf_op | source)
XLA Modules:
  0.0 1191.2 jit_solution(15400326370892282661)
XLA Ops:
  18.8 42.4 %all-reduce.19 = (bf16[768]{0:T(1024)(128)(2,1)S(1)}, bf16[768]{0:T(1024)(128)(2,1)S(1)}, bf16[768]{0:T(1024)(128)(2,1)S(1)}, bf16[768]{0:T(1024)(128)(2,1)S(1)}...) all-reduce(bf16[768]{0:T(1024)(128)(2,1)S(1)} %dynamic-update-slice, ...), channel_id=1, replica_groups=mesh['dp'=32] {'dp'}, use_global_device_ids=true, to_apply=%add | all-reduce | flops 9216 | bytes 36864
  61.9 4.3 copy.92
  67.5 2.4 copy.102
  71.2 4.0 add_convert_fusion.1
  75.2 2.4 copy.94
  77.6 4.1 reshape.151
  81.8 42.2 %all-gather.11.cloned.1.call-done = bf16[768,768]{1,0:T(8,128)(2,1)} async-done(((bf16[24,768]{1,0:T(8,128)(2,1)}), bf16[768,768]{1,0:T(8,128)(2,1)}) %all-gather.11.cloned.1.call-update) | async-done | bytes 1179664 | tf_op jit(solution)/shard_map/all_gather | solution.py:140
  124.0 5.4 convolution_convert_fusion.1
  129.3 4.3 copy.95
  133.7 5.2 reshape.152
  138.9 41.0 %all-gather.7.cloned.1.call-done = bf16[768,768]{1,0:T(8,128)(2,1)} async-done(((bf16[24,768]{1,0:T(8,128)(2,1)}), bf16[768,768]{1,0:T(8,128)(2,1)}) %all-gather.7.cloned.1.call-update) | async-done | bytes 1179664 | tf_op jit(solution)/shard_map/all_gather | solution.py:141
  179.9 5.4 add_convert_fusion.2
  185.3 4.3 copy.93
  189.5 5.2 reshape.150
  194.7 17.4 %fusion.62 = (f32[4,12,384]{2,1,0:T(8,128)S(1)}, f32[4,12,384,384]{2,3,1,0:T(8,128)}) fusion(pred[4,384]{1,0:T(4,128)(4,1)S(1)} %iota_compare_fusion.1, bf16[4,384,12,64]{1,0,3,2:T(4,128)(2,1)} %reshape.152, bf16[4,384,12,64]{1,0,3,2:T(4,128)(2,1)S(1)} %reshape.151), kind=kOutput, calls=%fused_computation.105 | convolution fusion | flops 934281600 | bytes 33105408 | tf_op jit(solution)/shard_map/sub | solution.py:74
  212.2 12.1 %convert_bitcast_fusion.1 = bf16[4,384,12,64]{1,3,2,0:T(8,128)(2,1)S(1)} fusion(bf16[4,384,12,64]{1,0,3,2:T(4,128)(2,1)} %reshape.150, f32[4,12,384,384]{2,3,1,0:T(8,128)} %get-tuple-element.102, f32[4,12,384]{2,1,0:T(8,128)S(1)} %get-tuple-element.101), kind=kOutput, calls=%fused_computation.68 | convolution fusion | flops 921305088 | bytes 33103872 | tf_op jit(solution)/shard_map/shij,sjhe->sihe/dot_general | solution.py:77
  224.3 1.8 copy.100
  226.6 9.1 all-gather.13.cloned.1.call-done
  235.6 4.5 fusion.71
  240.7 1.6 copy-done
  243.1 57.9 %all-gather.15.cloned.1.call-done = bf16[768,3072]{1,0:T(8,128)(2,1)} async-done(((bf16[24,3072]{1,0:T(8,128)(2,1)}), bf16[768,3072]{1,0:T(8,128)(2,1)}) %all-gather.15.cloned.1.call-update) | async-done | bytes 4718608 | tf_op jit(solution)/shard_map/all_gather | solution.py:151
  301.0 49.6 %multiply_convert_fusion.1 = (bf16[1536,3072]{1,0:T(8,128)(2,1)}, f32[1536,3072]{1,0:T(8,128)}, f32[1536,3072]{1,0:T(8,128)}) fusion(f32[3072]{0:T(1024)S(1)} %convert_element_type.152, bf16[768,3072]{1,0:T(8,128)(2,1)} %all-gather.15.cloned.1.call-done, bf16[1536,768]{0,1:T(8,128)(2,1)S(1)} %fusion.59.clone.4), kind=kOutput, calls=%fused_computation.10 | convolution fusion | flops 7559184384 | bytes 54276096 | tf_op jit(solution)/shard_map/dot_general | solution.py:95
  350.6 15.7 %all-gather.17.cloned.1.call-done = bf16[3072,768]{1,0:T(8,128)(2,1)} async-done(((bf16[96,768]{1,0:T(8,128)(2,1)}), bf16[3072,768]{1,0:T(8,128)(2,1)}) %all-gather.17.cloned.1.call-update) | async-done | bytes 4718608 | tf_op jit(solution)/shard_map/all_gather | solution.py:153
  366.2 13.5 %fusion.72 = (f32[1536]{0:T(1024)S(1)}, f32[1536,768]{0,1:T(8,128)S(1)}) fusion(f32[768]{0:T(1024)S(1)} %copy-done.34, bf16[1536,3072]{1,0:T(8,128)(2,1)} %get-tuple-element.98, bf16[3072,768]{1,0:T(8,128)(2,1)} %all-gather.17.cloned.1.call-done, f32[768]{0:T(1024)S(1)} %convert_element_type.150, f32[768]{0:T(1024)S(1)} %convert_element_type.149, ...), kind=kOutput, calls=%fused_computation.107 | convolution fusion | flops 7256013312 | bytes 23620608 | tf_op jit(solution)/shard_map/dot_general | solution.py:99
  381.4 3.3 multiply_reduce_fusion.1
  384.8 4.9 convert_reduce_fusion.1
  389.7 27.0 %convert_reduce_fusion = (f32[3072]{0:T(1024)}, bf16[1536,3072]{1,0:T(8,128)(2,1)}) fusion(f32[1536,3072]{1,0:T(8,128)} %get-tuple-element.99, bf16[1536,768]{0,1:T(8,128)(2,1)} %get-tuple-element.95, bf16[3072,768]{1,0:T(8,128)(2,1)} %all-gather.17.cloned.1.call-done, f32[1536,3072]{1,0:T(8,128)} %get-tuple-element.105, f32[3072]{0:T(1024)S(1)} %convert_element_type.152), kind=kOutput, calls=%fused_computation.8 | convolution fusion | flops 7327970304 | bytes 54288384 | tf_op jit(solution)/shard_map/rd,fd->rf/dot_general | solution.py:190
  416.6 15.6 %multiply_reduce_fusion.2 = (f32[768]{0:T(1024)}, f32[1536]{0:T(1024)S(1)}, f32[1536]{0:T(1024)S(1)}, f32[768]{0:T(1024)}, f32[1536,768]{0,1:T(8,128)S(1)}) fusion(f32[1536,768]{0,1:T(8,128)S(1)} %bitcast.82, f32[1536]{0:T(1024)S(1)} %add_rsqrt_fusion.1, f32[1536]{0:T(1024)S(1)} %broadcast_multiply_fusion.5, f32[768]{0:T(1024)S(1)} %convert_element_type.149, ...), kind=kOutput, calls=%fused_computation.34 | convolution fusion | flops 7270165504 | bytes 30738432 | tf_op jit(solution)/shard_map/rf,df->rd/dot_general | solution.py:201
  432.3 2.2 convert_reduce_fusion.2
  434.4 2.2 copy-done.2
  436.6 3.5 convolution_convert_fusion
  440.1 2.9 copy.104
  443.0 2.1 reshape.153
  445.1 14.1 %convert_reduce_fusion.3 = (f32[12,64]{1,0:T(8,128)S(1)}, bf16[4,384,12,64]{1,3,2,0:T(8,128)(2,1)}) fusion(f32[4,12,384,384]{2,3,1,0:T(8,128)} %get-tuple-element.102, f32[4,12,384]{2,1,0:T(8,128)S(1)} %copy-done.23, bf16[4,384,12,64]{1,0,3,2:T(4,128)(2,1)} %reshape.153), kind=kOutput, calls=%fused_computation.36 | convolution fusion | flops 923663616 | bytes 33106944 | tf_op jit(solution)/shard_map/shij,sihe->sjhe/dot_general | solution.py:253
  459.2 20.9 %multiply_reduce_fusion = (f32[4,12,384]{2,1,0:T(8,128)S(1)}, f32[4,12,384,384]{2,3,1,0:T(8,128)}) fusion(f32[4,12,384,384]{2,3,1,0:T(8,128)} %get-tuple-element.102, f32[4,12,384]{2,1,0:T(8,128)S(1)} %copy-done.23, bf16[4,384,12,64]{1,0,3,2:T(4,128)(2,1)S(1)} %copy-done.16, bf16[4,384,12,64]{1,0,3,2:T(4,128)(2,1)S(1)} %copy-done.19), kind=kOutput, calls=%fused_computation.2 | convolution fusion | flops 927184896 | bytes 61489152 | tf_op jit(solution)/shard_map/sihe,sjhe->shij/dot_general | solution.py:250
  480.0 3.6 copy.117
  484.1 1.4 copy-done.6
  485.5 2.0 convolution_bitcast_fusion
  487.5 2.0 copy.137
  489.6 24.3 %multiply_convert_fusion = bf16[4,12,384,384]{2,3,1,0:T(8,128)(2,1)} fusion(f32[4,12,384,384]{2,3,1,0:T(8,128)} %get-tuple-element.110, f32[4,12,384]{2,1,0:T(8,128)S(1)} %get-tuple-element.109, f32[4,12,384,384]{2,3,1,0:T(8,128)} %get-tuple-element.102, f32[4,12,384]{2,1,0:T(8,128)S(1)} %copy-done.23), kind=kLoop, calls=%fused_computation.1 | loop fusion | flops 28311552 | bytes 70926336 | tf_op jit(solution)/shard_map/convert_element_type | solution.py:258
  513.9 7.9 convert_reduce_fusion.4
  521.8 1.8 copy.109
  524.0 1.4 copy-done.14
  525.4 2.0 convolution_bitcast_fusion.2
  527.4 1.9 copy.133
  529.4 6.7 fusion.51
  536.4 11.5 fusion.22
  547.9 3.7 copy.113
  552.0 1.4 copy-done.17
  553.4 2.0 convolution_bitcast_fusion.1
  555.4 2.0 copy.135
  557.5 13.8 %fusion.56 = f32[768,3072]{1,0:T(8,128)} fusion(bf16[1536,3072]{1,0:T(8,128)(2,1)} %get-tuple-element.116, f32[1536,768]{0,1:T(8,128)} %copy-done, f32[768]{0:T(1024)S(1)} %copy-done.27, f32[768]{0:T(1024)S(1)} %convert_element_type.149, f32[1536]{0:T(1024)S(1)} %add_rsqrt_fusion.1, f32[1536]{0:T(1024)S(1)} %broadcast_multiply_fusion.5), kind=kOutput, calls=%fused_computation.103 | convolution fusion | flops 7253655552 | bytes 23611392 | tf_op jit(solution)/shard_map/rd,rf->df/dot_general | solution.py:198
  573.0 12.3 %fusion.73 = f32[3072,768]{1,0:T(8,128)} fusion(bf16[1536,3072]{1,0:T(8,128)(2,1)} %get-tuple-element.98, bf16[1536,768]{0,1:T(8,128)(2,1)S(1)} %copy-done.20), kind=kOutput, calls=%fused_computation.108 | convolution fusion | flops 7247757312 | bytes 21233664 | tf_op jit(solution)/shard_map/rf,rd->fd/dot_general | solution.py:187
  586.1 40.7 %all-reduce.18 = (f32[768]{0:T(1024)S(1)}, f32[768]{0:T(1024)S(1)}, f32[768]{0:T(1024)S(1)}, f32[768]{0:T(1024)S(1)}, f32[768]{0:T(1024)S(1)}, /*index=5*/f32[30...) all-reduce(f32[768]{0:T(1024)S(1)} %reduce_sum.206, ...), channel_id=6, replica_groups=mesh['dp'=32] {'dp'}, use_global_device_ids=true, to_apply=%region_16.17.clone | all-reduce | flops 9216 | bytes 73728
  631.5 3.4 fusion.74
  634.9 2.0 fusion.75
  637.0 4.3 add_add_fusion
  641.3 6.2 copy.120
  647.5 2.4 copy.119
  650.5 41.7 %reduce-scatter.19.cloned.1.call-done = f32[24,768]{1,0:T(8,128)} async-done(((f32[768,768]{1,0:T(8,128)}), f32[24,768]{1,0:T(8,128)}) %reduce-scatter.19.cloned.1.call-update) | async-done | bytes 73744
  692.2 103.9 %reduce-scatter.13.cloned.1.call-done = f32[24,768]{1,0:T(8,128)} async-done(((f32[768,768]{1,0:T(8,128)}), f32[24,768]{1,0:T(8,128)}) %reduce-scatter.13.cloned.1.call-update) | async-done | bytes 73744 | tf_op jit(solution)/shard_map/reduce_scatter | solution.py:282
  796.2 104.7 %reduce-scatter.21.cloned.1.call-done = f32[24,768]{1,0:T(8,128)} async-done(((f32[768,768]{1,0:T(8,128)}), f32[24,768]{1,0:T(8,128)}) %reduce-scatter.21.cloned.1.call-update) | async-done | bytes 73744
  900.9 141.1 %reduce-scatter.15.cloned.1.call-done = f32[24,3072]{1,0:T(8,128)} async-done(((f32[768,3072]{1,0:T(8,128)}), f32[24,3072]{1,0:T(8,128)}) %reduce-scatter.15.cloned.1.call-update) | async-done | bytes 294928 | tf_op jit(solution)/shard_map/reduce_scatter | solution.py:205
  1041.9 142.0 %reduce-scatter.17.cloned.1.call-done = f32[96,768]{1,0:T(8,128)} async-done(((f32[3072,768]{1,0:T(8,128)}), f32[96,768]{1,0:T(8,128)}) %reduce-scatter.17.cloned.1.call-update) | async-done | bytes 294928 | tf_op jit(solution)/shard_map/reduce_scatter | solution.py:207
  (167 shorter events, 27.4 us)
Async XLA Ops:
  7.2 60.3 %copy-start.9 = (bf16[1536,768]{1,0:T(8,128)(2,1)S(1)}, bf16[1536,768]{1,0:T(8,128)(2,1)}, u32[]{:S(2)}) copy-start(bf16[1536,768]{1,0:T(8,128)(2,1)} %param.37) | copy-start | bytes 7077892
  7.2 64.0 %all-gather.9.cloned.1.call-start = ((), (), s32[]{:S(2)}) async-start(), calls=%async_computation.7 | async-start | bytes 1216512 | tf_op jit(solution)/shard_map/all_gather | solution.py:139
  7.9 116.0 %all-gather.11.cloned.1.call-start = ((), (), s32[]{:S(2)}) async-start(), calls=%async_computation.8 | async-start | bytes 1216512 | tf_op jit(solution)/shard_map/all_gather | solution.py:140
  8.7 171.2 %all-gather.7.cloned.1.call-start = ((), (), s32[]{:S(2)}) async-start(), calls=%async_computation.6 | async-start | bytes 1216512 | tf_op jit(solution)/shard_map/all_gather | solution.py:141
  9.4 226.2 %all-gather.13.cloned.1.call-start = ((), (), s32[]{:S(2)}) async-start(), calls=%async_computation.9 | async-start | bytes 1216512 | tf_op jit(solution)/shard_map/all_gather | solution.py:142
  10.0 291.0 %all-gather.15.cloned.1.call-start = ((), (), s32[]{:S(2)}) async-start(), calls=%async_computation.10 | async-start | bytes 4866048 | tf_op jit(solution)/shard_map/all_gather | solution.py:151
  10.6 355.6 %all-gather.17.cloned.1.call-start = ((), (), s32[]{:S(2)}) async-start(), calls=%async_computation.11 | async-start | bytes 4866048 | tf_op jit(solution)/shard_map/all_gather | solution.py:153
  11.2 639.4 %reduce-scatter.23.cloned.1.call-start = ((), (), s32[]{:S(2)}) async-start(), calls=%async_computation.17 | async-start | bytes 2433024
  61.9 8.0 copy-start.39
  66.3 299.9 %copy-start.26 = (f32[768]{0:T(1024)}, f32[768]{0:T(1024)S(1)}, u32[]{:S(2)}) copy-start(f32[768]{0:T(1024)S(1)} %convert_element_type.150) | copy-start | bytes 9220
  81.8 112.9 %copy-start.3 = (bf16[4,384,12,64]{1,0,3,2:T(4,128)(2,1)}, bf16[4,384,12,64]{1,0,3,2:T(4,128)(2,1)S(1)}, u32[]{:S(2)}) copy-start(bf16[4,384,12,64]{1,0,3,2:T(4,128)(2,1)S(1)} %reshape.151) | copy-start | bytes 7077892
  212.1 12.2 %copy-start.22 = (f32[4,12,384]{2,1,0:T(8,128)}, f32[4,12,384]{2,1,0:T(8,128)S(1)}, u32[]{:S(2)}) copy-start(f32[4,12,384]{2,1,0:T(8,128)S(1)} %get-tuple-element.101) | copy-start | bytes 221188
  226.5 13.6 %copy-start.13 = (bf16[96,8,4,384]{3,1,2,0:T(8,128)(2,1)}, bf16[96,8,4,384]{3,1,2,0:T(8,128)(2,1)S(1)}, u32[]{:S(2)}) copy-start(bf16[96,8,4,384]{3,1,2,0:T(8,128)(2,1)S(1)} %copy.139) | copy-start | bytes 7077892
  240.1 2.2 copy-start
  243.0 123.2 %copy-start.34 = (f32[768]{0:T(1024)S(1)}, f32[768]{0:T(1024)}, u32[]{:S(2)}) copy-start(f32[768]{0:T(1024)} %convert_element_type.154) | copy-start | bytes 9220
  379.7 1.7 copy-start.1
  379.7 1.7 copy-start.24
  379.7 1.6 copy-start.25
  380.3 4.4 copy-start.28
  384.7 31.9 %slice-start = ((s8[4718592]{0:T(1024)(128)(4,1)}), s8[4194304]{0:T(1024)(128)(4,1)S(1)}, s32[]{:S(2)}) async-start(s8[4718592]{0:T(1024)(128)(4,1)} %bitcast.81), calls=%async_computation.18 | async-start | bytes 8388608
  389.7 27.0 %slice-start.1 = ((s8[4718592]{0:T(1024)(128)(4,1)}), s8[524288]{0:T(1024)(128)(4,1)S(1)}, s32[]{:S(2)}) async-start(s8[4718592]{0:T(1024)(128)(4,1)} %bitcast.81), calls=%async_computation.19 | async-start | bytes 1048576
  432.3 4.3 copy-start.38
  434.4 2.2 copy-start.2
  440.1 5.0 copy-start.23
  445.1 14.1 %copy-start.16 = (bf16[4,384,12,64]{1,0,3,2:T(4,128)(2,1)S(1)}, bf16[4,384,12,64]{1,0,3,2:T(4,128)(2,1)}, u32[]{:S(2)}) copy-start(bf16[4,384,12,64]{1,0,3,2:T(4,128)(2,1)} %reshape.150) | copy-start | bytes 7077892
  445.1 14.1 %copy-start.19 = (bf16[4,384,12,64]{1,0,3,2:T(4,128)(2,1)S(1)}, bf16[4,384,12,64]{1,0,3,2:T(4,128)(2,1)}, u32[]{:S(2)}) copy-start(bf16[4,384,12,64]{1,0,3,2:T(4,128)(2,1)} %reshape.153) | copy-start | bytes 7077892
  480.0 5.5 copy-start.10
  484.1 1.4 copy-start.6
  489.5 202.7 %reduce-scatter.19.cloned.1.call-start = ((), (), s32[]{:S(2)}) async-start(), calls=%async_computation.15 | async-start | bytes 2433024
  489.5 24.3 %copy-start.8 = (bf16[4,384,12,64]{1,0,3,2:T(4,128)(2,1)S(1)}, bf16[4,384,12,64]{1,0,3,2:T(4,128)(2,1)}, u32[]{:S(2)}) copy-start(bf16[4,384,12,64]{1,0,3,2:T(4,128)(2,1)} %reshape.152) | copy-start | bytes 7077892
  521.7 3.6 copy-start.11
  524.0 1.4 copy-start.14
  529.3 7.0 copy-start.4
  529.4 266.8 %reduce-scatter.13.cloned.1.call-start = ((), (), s32[]{:S(2)}) async-start(), calls=%async_computation.12 | async-start | bytes 2433024 | tf_op jit(solution)/shard_map/reduce_scatter | solution.py:282
  536.1 364.7 %reduce-scatter.21.cloned.1.call-start = ((), (), s32[]{:S(2)}) async-start(), calls=%async_computation.16 | async-start | bytes 2433024
  547.9 5.5 copy-start.12
  552.0 1.4 copy-start.17
  555.4 2.1 copy-start.27
  557.5 484.5 %reduce-scatter.15.cloned.1.call-start = ((), (), s32[]{:S(2)}) async-start(), calls=%async_computation.13 | async-start | bytes 9732096 | tf_op jit(solution)/shard_map/reduce_scatter | solution.py:205
  571.4 1.7 copy-start.20
  571.4 612.5 %reduce-scatter.17.cloned.1.call-start = ((), (), s32[]{:S(2)}) async-start(), calls=%async_computation.14 | async-start | bytes 9732096 | tf_op jit(solution)/shard_map/reduce_scatter | solution.py:207
  585.3 0.7 copy-start.29
  585.4 0.7 copy-start.30
  585.4 0.7 copy-start.31
  585.4 0.7 copy-start.32
  585.4 0.7 copy-start.33
  585.4 0.7 copy-start.35
  585.4 0.7 copy-start.36
  585.4 46.1 %copy-start.15 = (bf16[96,8,4,384]{3,1,2,0:T(8,128)(2,1)S(1)}, bf16[96,8,4,384]{3,1,2,0:T(8,128)(2,1)}, u32[]{:S(2)}) copy-start(bf16[96,8,4,384]{3,1,2,0:T(8,128)(2,1)} %copy-done.14) | copy-start | bytes 7077892
  631.4 3.4 copy-start.18
  631.4 3.4 copy-start.37
  631.4 5.5 slice-start.2
  634.9 2.0 slice-start.3
  634.9 2.0 copy-start.7
  634.9 2.1 copy-start.21
  641.3 6.2 copy-start.5
Sparse Core Ops, SparseCore 0:
  10.9 56.9 all-gather.8
  70.8 53.1 all-gather.10
  126.9 52.9 all-gather.6
  182.6 52.9 all-gather.12
  238.4 62.5 all-gather.14
  303.7 62.4 all-gather.16
  489.6 97.8 reduce-scatter.22
  594.3 97.9 reduce-scatter.18
  698.1 98.0 reduce-scatter.12
  802.7 98.0 reduce-scatter.20
  907.3 134.5 reduce-scatter.14
  1049.3 134.5 reduce-scatter.16
where the time goes:
time: 1200 us; the launch traced here: 1190 us
  waiting for transfers between devices  703 us (59%)
  matrix products  261 us (22%)
  local copies, waits for them, and re-layouts  89.1 us (7%)
  blocking collectives  83.1 us (7%)
  other arithmetic  39.2 us (3%)
  between operations  15.2 us (1%)
    unnamed x15, waiting for transfers between devices  150 us
    reduce_scatter x1, waiting for transfers between devices, body(): lax.psum_scatter(grad_w_shrink, 'dp', scatter_dimension=0, tiled=True)  142 us
    reduce_scatter x1, waiting for transfers between devices, body(): lax.psum_scatter(grad_w_expand, 'dp', scatter_dimension=0, tiled=True)  141 us
    reduce_scatter x1, waiting for transfers between devices, body(): lax.psum_scatter(grad_w_output, 'dp', scatter_dimension=0, tiled=True)  104 us
    unnamed x2, blocking collectives  83.1 us
    all_gather x1, waiting for transfers between devices, body(): lax.all_gather(w_expand, 'dp', axis=0, tiled=True)  57.9 us
    dot_general x1, matrix products, ffn_forward(): jnp.dot(first_low, full_expand, preferred_element_type=jnp.float32)  49.6 us
    unnamed x126, local copies, waits for them, and re-layouts  46.8 us
  transfers between devices with their start and end apart: 12, of which 10 were waited for; matrix products, arithmetic and copies ran while one was open for 22% of the time, Pallas kernels for 0%

commit v1 on v0

v1 whole, which is shorter than its diff:
```python
import functools, math
import jax, jax.numpy as jnp
from jax import lax
from jax.experimental import pallas as pl
from jax.experimental.pallas import tpu as pltpu
from jax.sharding import PartitionSpec as P
BF=jnp.bfloat16; F32=jnp.float32
D=768; HD=64; PAIRS=6
VM=58<<20
NEG=-1e30
def mm(a,b): return lax.dot_general(a,b,(((1,),(0,)),((),())),preferred_element_type=F32)
def nt(a,b): return lax.dot_general(a,b,(((1,),(1,)),((),())),preferred_element_type=F32)
def tn(a,b): return lax.dot_general(a,b,(((0,),(0,)),((),())),preferred_element_type=F32)
def lanes(rows,n=128): return lax.broadcasted_iota(jnp.int32,(rows,n),1)

def attn_fwd_kernel(len_ref, x_ref, wq_ref, wk_ref, wv_ref, sp_ref, q_ref, k_ref, v_ref, c_ref, e_ref):
    L=x_ref.shape[0]
    s=pl.program_id(0)
    n=len_ref[s]
    x=x_ref[...]
    q=(mm(x,wq_ref[...])+sp_ref[6:7].astype(F32)).astype(BF)
    k=mm(x,wk_ref[...]).astype(BF)
    v=(mm(x,wv_ref[...])+sp_ref[7:8].astype(F32)).astype(BF)
    q_ref[...]=q; k_ref[...]=k; v_ref[...]=v
    ln=lanes(L)
    even=ln<64
    row=lax.broadcasted_iota(jnp.int32,(L,128),0)
    kx=jnp.where((ln==0)&(row>=n),NEG,0.0).astype(BF)
    qx=jnp.where(ln==0,1.0,0.0).astype(BF)
    one_e=jnp.where(even,1.0,0.0).astype(BF)
    one_o=jnp.where(even,0.0,1.0).astype(BF)
    zero=jnp.zeros((L,128),BF)
    mt=jnp.zeros((L,128),F32); lt=jnp.ones((L,128),F32)
    for t in range(PAIRS):
        cs=slice(128*t,128*t+128)
        qp=q[:,cs]*jnp.asarray(0.125,BF); kp=k[:,cs]; vp=v[:,cs]
        ke=jnp.concatenate([kp,kx],1)
        ps=[];ms=[]
        for o in (0,1):
            qm=jnp.where(even if o==0 else ~even, qp, zero)
            sc=nt(jnp.concatenate([qm,qx],1),ke)
            m=jnp.max(sc,1,keepdims=True)
            ps.append(jnp.exp(sc-m).astype(BF)); ms.append(m)
        vv=jnp.concatenate([jnp.concatenate([jnp.where(even,vp,zero),one_e],1),
                            jnp.concatenate([jnp.where(even,zero,vp),one_o],1)],0)
        r=mm(jnp.concatenate(ps,1),vv)
        lb=r[:,128:]
        c_ref[:,cs]=(r[:,:128]/lb).astype(BF)
        sel_e=ln==t; sel_o=ln==64+t
        mt=jnp.where(sel_e,ms[0],jnp.where(sel_o,ms[1],mt))
        lt=jnp.where(sel_e|sel_o,lb,lt)
    neg=-(mt+jnp.log(lt))
    hi=neg.astype(BF); r1=neg-hi.astype(F32)
    mid=r1.astype(BF); lo=(r1-mid.astype(F32)).astype(BF)
    use=(ln%64)<PAIRS
    z=jnp.zeros((L,128),F32)
    e=jnp.where(use,hi.astype(F32),z)+pltpu.roll(jnp.where(use,mid.astype(F32),z),8,1)+pltpu.roll(jnp.where(use,lo.astype(F32),z),16,1)
    e=jnp.where(ln==24,1.0,e)
    e_ref[...]=e.astype(BF)

def attn_fwd(lengths,x,wq,wk,wv,sp):
    S=lengths.shape[0]; R=x.shape[0]; L=R//S
    rowb=pl.BlockSpec((L,D),lambda s,*_:(s,0))
    w=pl.BlockSpec((D,D),lambda s,*_:(0,0))
    b=pl.BlockSpec((8,D),lambda s,*_:(0,0))
    return pl.pallas_call(attn_fwd_kernel,
        grid_spec=pltpu.PrefetchScalarGridSpec(num_scalar_prefetch=1,grid=(S,),
            in_specs=[rowb,w,w,w,b],
            out_specs=[rowb,rowb,rowb,rowb,pl.BlockSpec((L,128),lambda s,*_:(s,0))]),
        out_shape=[jax.ShapeDtypeStruct((R,D),BF)]*4+[jax.ShapeDtypeStruct((R,128),BF)],
        compiler_params=pltpu.CompilerParams(vmem_limit_bytes=VM),
        cost_estimate=pl.CostEstimate(flops=9_000_000_000,bytes_accessed=20_000_000,transcendentals=7_000_000),
        name="attn_fwd")(lengths,x,wq,wk,wv,sp)

def attn_bwd_kernel(len_ref, q_ref, k_ref, v_ref, c_ref, e_ref, g_ref, dq_ref, dk_ref, dv_ref, sm_ref):
    L=q_ref.shape[0]
    s=pl.program_id(0)
    n=len_ref[s]
    ln=lanes(L); even=ln<64
    row=lax.broadcasted_iota(jnp.int32,(L,128),0)
    eq=e_ref[...]
    mask=(ln==24)&(row>=n)
    zero=jnp.zeros((L,128),BF); zf=jnp.zeros((L,128),F32)
    scale=jnp.asarray(0.125,BF)
    kbase=jnp.where(mask,NEG,0.0)
    for t in range(PAIRS):
        cs=slice(128*t,128*t+128)
        q=q_ref[:,cs]; k=k_ref[:,cs]; v=v_ref[:,cs]; g=g_ref[:,cs]
        qs=q*scale
        gc=g.astype(F32)*c_ref[:,cs].astype(F32)
        ps=[];ss=[]
        for o in (0,1):
            sel=even if o==0 else ~even
            d=jnp.sum(jnp.where(sel,gc,zf),1,keepdims=True)
            dh=d.astype(BF).astype(F32); dl=d-dh
            gx=jnp.where(ln==0,-dh,jnp.where(ln==1,-dl,zf)).astype(BF)
            base=64*o+t
            hot=(ln==base)|(ln==base+8)|(ln==base+16)
            kx=jnp.where(hot,1.0,kbase).astype(BF)
            vx=jnp.where(ln<2,1.0,0.0).astype(BF)
            sc=nt(jnp.concatenate([jnp.where(sel,qs,zero),eq],1),jnp.concatenate([k,kx],1))
            p=jnp.exp(sc)
            dp=nt(jnp.concatenate([jnp.where(sel,g,zero),gx],1),jnp.concatenate([v,vx],1))
            ds=(p*dp).astype(BF)
            ps.append(p.astype(BF)); ss.append(ds)
        kk=jnp.concatenate([jnp.where(even,k,zero),jnp.where(even,zero,k)],0)
        dq_ref[:,cs]=(mm(jnp.concatenate(ss,1),kk)*0.125).astype(BF)
        qq=jnp.concatenate([jnp.where(even,q,zero),jnp.where(even,zero,q)],0)
        gg=jnp.concatenate([jnp.where(even,g,zero),jnp.where(even,zero,g)],0)
        dk_ref[:,cs]=(tn(jnp.concatenate(ss,0),qq)*0.125).astype(BF)
        dv_ref[:,cs]=tn(jnp.concatenate(ps,0),gg).astype(BF)
    u=jnp.concatenate([colsum(dq_ref[...].astype(F32)),colsum(dv_ref[...].astype(F32)),jnp.zeros((6,D),F32)],0)
    @pl.when(s==0)
    def _(): sm_ref[...]=u
    @pl.when(s>0)
    def _(): sm_ref[...]+=u

def attn_bwd(lengths,q,k,v,c,e,g):
    S=lengths.shape[0]; R=q.shape[0]; L=R//S
    rowb=pl.BlockSpec((L,D),lambda s,*_:(s,0))
    w=pl.BlockSpec((D,D),lambda s,*_:(0,0))
    return pl.pallas_call(attn_bwd_kernel,
        grid_spec=pltpu.PrefetchScalarGridSpec(num_scalar_prefetch=1,grid=(S,),
            in_specs=[rowb,rowb,rowb,rowb,pl.BlockSpec((L,128),lambda s,*_:(s,0)),rowb],
            out_specs=[rowb,rowb,rowb,pl.BlockSpec((8,D),lambda s,*_:(0,0))]),
        out_shape=[jax.ShapeDtypeStruct((R,D),BF)]*3+[jax.ShapeDtypeStruct((8,D),F32)],
        compiler_params=pltpu.CompilerParams(vmem_limit_bytes=VM),
        cost_estimate=pl.CostEstimate(flops=15_000_000_000,bytes_accessed=24_000_000,transcendentals=7_000_000),
        name="attn_bwd")(lengths,q,k,v,c,e,g)

EPS=1e-12
def gelu_parts(v):
    a=jnp.abs(v)
    d=1.0+a*(0.3275911*math.sqrt(0.5))
    t=pl.reciprocal(d,approx=True)
    t=t*(2.0-d*t)
    ex=jnp.exp(v*v*-0.5)
    po=((((1.061405429*0.5*t-1.453152027*0.5)*t+1.421413741*0.5)*t-0.284496736*0.5)*t+0.254829592*0.5)*t
    tail=po*ex
    phi=jnp.where(v>=0,1.0-tail,tail)
    return v*phi, phi+v*(ex*(1.0/math.sqrt(2*math.pi)))
def ln_parts(h):
    mu=jnp.mean(h,1,keepdims=True); c=h-mu
    r=lax.rsqrt(jnp.mean(c*c,1,keepdims=True)+EPS)
    return c*r, r
def ln_back(up,n,r,gain):
    e=up*gain
    return r*(e-jnp.mean(e,1,keepdims=True)-n*jnp.mean(e*n,1,keepdims=True))
def colsum(x): return jnp.sum(x,0,keepdims=True)
FC=512
def ffn_fwd_kernel(bk_ref,x_ref,c_ref,go_ref,wo_ref,we_ref,ws_ref,sp_ref,be_ref,
        n1_ref,r1_ref,fl_ref,act_ref,gp_ref,out_ref,gh_ref,gs_ref,sm_ref):
    M=x_ref.shape[0]; FF=we_ref.shape[1]
    s=pl.program_id(0)
    sp=sp_ref[...].astype(F32)
    bo,g1,s1,bs,g2,s2=[sp[i:i+1] for i in range(6)]
    att=mm(c_ref[...],wo_ref[...])+bo
    n1,r1=ln_parts(x_ref[...].astype(F32)+att)
    n1_ref[...]=n1; r1_ref[...]=jnp.broadcast_to(r1,(M,128))
    first=n1*g1+s1
    fl=first.astype(BF); fl_ref[...]=fl
    acc=jnp.zeros((M,D),F32)
    for f in range(0,FF,FC):
        fs=slice(f,f+FC)
        ex=mm(fl,we_ref[:,fs])+be_ref[:,fs].astype(F32)
        a,gp=gelu_parts(ex)
        ab=a.astype(BF)
        act_ref[:,fs]=ab; gp_ref[:,fs]=gp.astype(BF)
        acc=acc+mm(ab,ws_ref[fs,:])
    n2,r2=ln_parts(first+(acc+bs))
    rows=jnp.where(bk_ref[s]==0,176,jnp.where(bk_ref[s]==1,224,384))
    rm=jnp.where(lax.broadcasted_iota(jnp.int32,(M,1),0)<rows,1.0,0.0)
    out_ref[...]=((n2*g2+s2)*rm).astype(BF)
    up=go_ref[...].astype(F32)*rm
    gh=ln_back(up,n2,r2,g2)
    gh_ref[...]=gh
    gs=gh.astype(BF); gs_ref[...]=gs
    u=jnp.concatenate([colsum(up*n2),colsum(up),colsum(gs.astype(F32)),jnp.zeros((5,D),F32)],0)
    @pl.when(s==0)
    def _(): sm_ref[...]=u
    @pl.when(s>0)
    def _(): sm_ref[...]+=u

def ffn_fwd(buckets,x,c,go,wo,we,ws,sp,be):
    S=buckets.shape[0]; R=x.shape[0]; M=R//S; FF=we.shape[1]
    rb=lambda n:pl.BlockSpec((M,n),lambda s,*_:(s,0))
    full=lambda a,b:pl.BlockSpec((a,b),lambda s,*_:(0,0))
    return pl.pallas_call(ffn_fwd_kernel,
        grid_spec=pltpu.PrefetchScalarGridSpec(num_scalar_prefetch=1,grid=(S,),
            in_specs=[rb(D),rb(D),rb(D),full(D,D),full(D,FF),full(FF,D),full(8,D),full(1,FF)],
            out_specs=[rb(D),rb(128),rb(D),rb(FF),rb(FF),rb(D),rb(D),rb(D),full(8,D)]),
        out_shape=[jax.ShapeDtypeStruct((R,D),F32),jax.ShapeDtypeStruct((R,128),F32),jax.ShapeDtypeStruct((R,D),BF),
            jax.ShapeDtypeStruct((R,FF),BF),jax.ShapeDtypeStruct((R,FF),BF),jax.ShapeDtypeStruct((R,D),BF),
            jax.ShapeDtypeStruct((R,D),F32),jax.ShapeDtypeStruct((R,D),BF),jax.ShapeDtypeStruct((8,D),F32)],
        compiler_params=pltpu.CompilerParams(vmem_limit_bytes=VM),
        cost_estimate=pl.CostEstimate(flops=17_000_000_000,bytes_accessed=60_000_000,transcendentals=9_000_000),
        name="ffn_fwd")(buckets,x,c,go,wo,we,ws,sp,be)

def ffn_bwd_kernel(gs_ref,gh_ref,gp_ref,n1_ref,r1_ref,wo_ref,we_ref,ws_ref,sp_ref,
        ge_ref,gr_ref,ga_ref,gc_ref,sm_ref,sb_ref):
    M=gs_ref.shape[0]; FF=we_ref.shape[1]
    s=pl.program_id(0)
    g1=sp_ref[1:2].astype(F32)
    gs=gs_ref[...]
    acc=gh_ref[...]
    bsum=[]
    for f in range(0,FF,FC):
        fs=slice(f,f+FC)
        ge=(nt(gs,ws_ref[fs,:])*gp_ref[:,fs].astype(F32)).astype(BF)
        ge_ref[:,fs]=ge
        bsum.append(colsum(ge.astype(F32)))
        acc=acc+nt(ge,we_ref[:,fs])
    n1=n1_ref[...]
    gr=ln_back(acc,n1,r1_ref[:,:1],g1)
    gr_ref[...]=gr
    ga=gr.astype(BF); ga_ref[...]=ga
    gc_ref[...]=nt(ga,wo_ref[...]).astype(BF)
    u=jnp.concatenate([colsum(ga.astype(F32)),colsum(acc*n1),colsum(acc),jnp.zeros((5,D),F32)],0)
    ub=jnp.concatenate(bsum,1)
    @pl.when(s==0)
    def _():
        sm_ref[...]=u; sb_ref[...]=ub
    @pl.when(s>0)
    def _():
        sm_ref[...]+=u; sb_ref[...]+=ub

def ffn_bwd(gs,gh,gp,n1,r1,wo,we,ws,sp,S):
    R=gs.shape[0]; M=R//S; FF=we.shape[1]
    rb=lambda n:pl.BlockSpec((M,n),lambda s:(s,0))
    full=lambda a,b:pl.BlockSpec((a,b),lambda s:(0,0))
    return pl.pallas_call(ffn_bwd_kernel,grid=(S,),
            in_specs=[rb(D),rb(D),rb(FF),rb(D),rb(128),full(D,D),full(D,FF),full(FF,D),full(8,D)],
            out_specs=[rb(FF),rb(D),rb(D),rb(D),full(8,D),full(1,FF)],
        out_shape=[jax.ShapeDtypeStruct((R,FF),BF),jax.ShapeDtypeStruct((R,D),F32),jax.ShapeDtypeStruct((R,D),BF),
            jax.ShapeDtypeStruct((R,D),BF),jax.ShapeDtypeStruct((8,D),F32),jax.ShapeDtypeStruct((1,FF),F32)],
        compiler_params=pltpu.CompilerParams(vmem_limit_bytes=VM),
        cost_estimate=pl.CostEstimate(flops=17_000_000_000,bytes_accessed=60_000_000,transcendentals=0),
        name="ffn_bwd")(gs,gh,gp,n1,r1,wo,we,ws,sp)

def tn_kernel(a_ref,b_ref,o_ref): o_ref[...]=tn(a_ref[...],b_ref[...]).astype(o_ref.dtype)
def grad_w(a,b,bm,bn,name,dt=BF,order=0):
    R,Ma=a.shape; Nb=b.shape[1]
    if order==0:
        grid=(Ma//bm,Nb//bn); ia=lambda i,j:(0,i); ib=lambda i,j:(0,j); io=lambda i,j:(i,j)
    else:
        grid=(Nb//bn,Ma//bm); ia=lambda j,i:(0,i); ib=lambda j,i:(0,j); io=lambda j,i:(i,j)
    return pl.pallas_call(tn_kernel,grid=grid,in_specs=[pl.BlockSpec((R,bm),ia),pl.BlockSpec((R,bn),ib)],
        out_specs=pl.BlockSpec((bm,bn),io),out_shape=jax.ShapeDtypeStruct((Ma,Nb),dt),
        compiler_params=pltpu.CompilerParams(vmem_limit_bytes=VM),
        cost_estimate=pl.CostEstimate(flops=2*R*Ma*Nb,bytes_accessed=2*R*(Ma+Nb)+2*Ma*Nb,transcendentals=0),
        name=name)(a,b)
def resid_kernel(gr_ref,a_ref,b_ref,c_ref,wa_ref,wb_ref,wc_ref,o_ref):
    o_ref[...]=gr_ref[...]+nt(a_ref[...],wa_ref[...])+nt(b_ref[...],wb_ref[...])+nt(c_ref[...],wc_ref[...])
def grad_in(gr,a,b,c,wa,wb,wc,S):
    R=gr.shape[0]; M=R//S
    rb=pl.BlockSpec((M,D),lambda s:(s,0)); w=pl.BlockSpec((D,D),lambda s:(0,0))
    return pl.pallas_call(resid_kernel,grid=(S,),in_specs=[rb]*4+[w]*3,out_specs=rb,
        out_shape=jax.ShapeDtypeStruct((R,D),F32),
        compiler_params=pltpu.CompilerParams(vmem_limit_bytes=VM),
        cost_estimate=pl.CostEstimate(flops=6*R*D*D,bytes_accessed=20_000_000,transcendentals=0),
        name="grad_in")(gr,a,b,c,wa,wb,wc)


def exchange(value, pairs):
    return lax.ppermute(value, "dp", pairs)


def flip(count, mask):
    return [(i, i ^ mask) for i in range(count)]


def turn(count, even_mask, odd_mask):
    return [(i, i ^ (odd_mask if i & 1 else even_mask)) for i in range(count)]


def gather_tree(block):
    along_z = jnp.stack([block] + [exchange(block, flip(32, 8 * k)) for k in (1, 2, 3)])
    near = exchange(along_z, turn(32, 2, 4))
    far = exchange(jnp.concatenate([along_z, near]), turn(32, 4, 2))
    mine = (along_z, near, far)
    return mine + tuple(exchange(piece, flip(32, 1)) for piece in mine)


def piece_owner(me, other_core, far, near, k):
    core = me & 1
    near_mask = 2 + 2 * (core ^ other_core)
    far_mask = 6 - near_mask
    return me ^ (other_core + far * far_mask + near * near_mask + 8 * k)


def unpack_kernel(cuts, me_ref, *refs):
    pieces, outs, sems = refs[:6], refs[6:-1], refs[-1]
    me = me_ref[0]
    for other in (0, 1):
        along_z, near, far = pieces[3 * other : 3 * other + 3]
        for k in range(4):
            for ref, at, owner in (
                (along_z, k, piece_owner(me, other, 0, 0, k)),
                (near, k, piece_owner(me, other, 0, 1, k)),
                (far, k, piece_owner(me, other, 1, 0, k)),
                (far, 4 + k, piece_owner(me, other, 1, 1, k)),
            ):
                for i, (start, rows) in enumerate(cuts):
                    pltpu.make_async_copy(
                        ref.at[at, pl.ds(start, rows)], outs[i].at[owner], sems.at[i]
                    ).start()
    for i, out in enumerate(outs):
        pltpu.make_async_copy(out, out, sems.at[i]).wait()


def unpack(me, pieces, heights, name):
    cuts = []
    start = 0
    for rows in heights:
        cuts.append((start, rows))
        start += rows
    anywhere = pl.BlockSpec(memory_space=pl.ANY)
    return pl.pallas_call(
        functools.partial(unpack_kernel, tuple(cuts)),
        grid_spec=pltpu.PrefetchScalarGridSpec(
            num_scalar_prefetch=1,
            grid=(1,),
            in_specs=[anywhere] * 6,
            out_specs=[anywhere] * len(cuts),
            scratch_shapes=[pltpu.SemaphoreType.DMA((len(cuts),))],
        ),
        out_shape=[jax.ShapeDtypeStruct((32, rows, D), BF) for rows in heights],
        compiler_params=pltpu.CompilerParams(vmem_limit_bytes=4 << 20),
        cost_estimate=pl.CostEstimate(
            flops=0, bytes_accessed=2 * 64 * D * start, transcendentals=0
        ),
        name=name,
    )(me, *pieces)


def pack_kernel(cuts, me_ref, *refs):
    sources, (keep, send, sems) = refs[:-3], refs[-3:]
    me = me_ref[0]
    for other, target in ((0, keep), (1, send)):
        for far in (0, 1):
            for near in (0, 1):
                for k in range(4):
                    owner = piece_owner(me, other, far, near, k)
                    for i, start, rows, column in cuts:
                        pltpu.make_async_copy(
                            sources[i].at[owner, :, pl.ds(column, D)],
                            target.at[8 * far + 4 * near + k, pl.ds(start, rows)],
                            sems.at[other],
                        ).start()
    for other, target in ((0, keep), (1, send)):
        pltpu.make_async_copy(target, target, sems.at[other]).wait()


def pack(me, sources, name):
    cuts = []
    start = 0
    for i, source in enumerate(sources):
        for column in range(0, source.shape[2], D):
            cuts.append((i, start, source.shape[1], column))
            start += source.shape[1]
    anywhere = pl.BlockSpec(memory_space=pl.ANY)
    return pl.pallas_call(
        functools.partial(pack_kernel, tuple(cuts)),
        grid_spec=pltpu.PrefetchScalarGridSpec(
            num_scalar_prefetch=1,
            grid=(1,),
            in_specs=[anywhere] * len(sources),
            out_specs=[anywhere] * 2,
            scratch_shapes=[pltpu.SemaphoreType.DMA((2,))],
        ),
        out_shape=[jax.ShapeDtypeStruct((16, start, D), BF)] * 2,
        compiler_params=pltpu.CompilerParams(vmem_limit_bytes=4 << 20),
        cost_estimate=pl.CostEstimate(
            flops=0, bytes_accessed=2 * 64 * D * start, transcendentals=0
        ),
        name=name,
    )(me, *sources)


def add_up(*parts):
    total = parts[0].astype(F32)
    for part in parts[1:]:
        total = total + part.astype(F32)
    return total


def scatter_tree(keep, send):
    came = exchange(send, flip(32, 1))
    low = add_up(keep[:8], came[:8]).astype(BF)
    high = add_up(keep[8:], came[8:]).astype(BF)
    came = exchange(high, turn(32, 4, 2))
    high = add_up(low[4:], came[4:]).astype(BF)
    low = add_up(low[:4], came[:4]).astype(BF)
    came = exchange(high, turn(32, 2, 4))
    sums = [add_up(low[k], came[k]).astype(BF) for k in range(4)]
    return add_up(sums[0], *[exchange(sums[k], flip(32, 8 * k)) for k in (1, 2, 3)])


def vector_row(vectors):
    row = jnp.concatenate(vectors)
    return jnp.pad(row[None], ((0, 7), (0, D - row.shape[0])))


def body(
    tokens,
    buckets,
    lengths,
    w_query,
    w_key,
    w_value,
    w_output,
    bias_query,
    bias_value,
    bias_output,
    gain_first,
    shift_first,
    w_expand,
    bias_expand,
    w_shrink,
    bias_shrink,
    gain_second,
    shift_second,
    grad_out,
    count,
):
    slots = buckets.shape[0]
    whole = lambda v: lax.all_gather(v, "dp", axis=0, tiled=True)
    short = (
        bias_output,
        gain_first,
        shift_first,
        bias_shrink,
        gain_second,
        shift_second,
        bias_query,
        bias_value,
    )
    tree = count == 32
    if tree:
        me = lax.axis_index("dp").astype(jnp.int32).reshape(1)
        first_block = jnp.concatenate(
            [w_query, w_key, w_value, vector_row(short + (bias_expand,))]
        )
        full_query, full_key, full_value, rows = unpack(
            me, gather_tree(first_block), (24, 24, 24, 8), "unpack_qkv"
        )
        full_query, full_key, full_value = [
            w.reshape(D, D) for w in (full_query, full_key, full_value)
        ]
        rows = rows[:, 0, :288]
        vectors = rows[:, :192].reshape(32, 8, 24).transpose(1, 0, 2).reshape(8, D)
        full_bias_expand = rows[:, 192:].reshape(1, 4 * D)
        full_output, full_shrink = unpack(
            me,
            gather_tree(jnp.concatenate([w_output, w_shrink])),
            (24, 96),
            "unpack_shrink",
        )
        full_output = full_output.reshape(D, D)
        full_shrink = full_shrink.reshape(4 * D, D)
        full_expand = whole(w_expand)
    else:
        full_query, full_key, full_value, full_output, full_expand, full_shrink = [
            whole(w) for w in (w_query, w_key, w_value, w_output, w_expand, w_shrink)
        ]
        vectors = jnp.stack([whole(v) for v in short])
        full_bias_expand = whole(bias_expand)[None]

    q, k, v, context, ends = attn_fwd(
        lengths, tokens, full_query, full_key, full_value, vectors
    )
    normed, root, first_low, active, slope, layer_out, grad_h2, grad_shrink, sums_a = ffn_fwd(
        buckets,
        tokens,
        context,
        grad_out,
        full_output,
        full_expand,
        full_shrink,
        vectors,
        full_bias_expand,
    )
    dw_shrink = grad_w(active, grad_shrink, 768, 768, "dw_shrink")
    grad_expand, grad_h1, grad_attended, grad_context, sums_b, d_bias_expand = ffn_bwd(
        grad_shrink,
        grad_h2,
        slope,
        normed,
        root,
        full_output,
        full_expand,
        full_shrink,
        vectors,
        slots,
    )
    dw_expand = grad_w(first_low, grad_expand, 768, 768, "dw_expand")
    dw_output = grad_w(context, grad_attended, 768, 384, "dw_output")
    dq, dk, dv, sums_c = attn_bwd(lengths, q, k, v, context, ends, grad_context)
    dw_query = grad_w(tokens, dq, 768, 384, "dw_query")
    dw_key = grad_w(tokens, dk, 768, 384, "dw_key")
    dw_value = grad_w(tokens, dv, 768, 384, "dw_value")
    grad_tokens = grad_in(
        grad_h1, dq, dk, dv, full_query, full_key, full_value, slots
    )
    sums = (
        sums_b[0],
        sums_b[1],
        sums_b[2],
        sums_a[2],
        sums_a[0],
        sums_a[1],
        sums_c[0],
        sums_c[1],
    )
    if tree:
        sum_shrink = scatter_tree(
            *pack(me, [dw_shrink.reshape(32, 96, D)], "pack_shrink")
        )
        sum_expand = scatter_tree(
            *pack(
                me,
                [dw_expand.reshape(32, 24, 4 * D), dw_output.reshape(32, 24, D)],
                "pack_expand",
            )
        )
        rows = jnp.stack(sums).reshape(8, 32, 24).transpose(1, 0, 2).reshape(32, 192)
        rows = jnp.concatenate([rows, d_bias_expand.reshape(32, 96)], 1).astype(BF)
        rows = jnp.pad(rows[:, None], ((0, 0), (0, 7), (0, D - 288)))
        sum_qkv = scatter_tree(
            *pack(
                me,
                [w.reshape(32, 24, D) for w in (dw_query, dw_key, dw_value)] + [rows],
                "pack_qkv",
            )
        )
        own_query, own_key, own_value = [sum_qkv[24 * i : 24 * i + 24] for i in range(3)]
        own_output = sum_expand[96:]
        own_expand = jnp.concatenate([sum_expand[24 * i : 24 * i + 24] for i in range(4)], 1)
        own_shrink = sum_shrink
        own_rows = sum_qkv[72]
        own_short = [own_rows[24 * i : 24 * i + 24] for i in range(8)]
        own_bias_expand = own_rows[192:288]
    else:
        owned = lambda v: lax.psum_scatter(
            v.astype(F32), "dp", scatter_dimension=0, tiled=True
        )
        own_query, own_key, own_value, own_output, own_expand, own_shrink = [
            owned(w)
            for w in (dw_query, dw_key, dw_value, dw_output, dw_expand, dw_shrink)
        ]
        own_short = [owned(v) for v in sums]
        own_bias_expand = owned(d_bias_expand[0])
    (
        own_bias_output,
        own_gain_first,
        own_shift_first,
        own_bias_shrink,
        own_gain_second,
        own_shift_second,
        own_bias_query,
        own_bias_value,
    ) = own_short
    return (
        layer_out,
        grad_tokens,
        own_query,
        own_key,
        own_value,
        own_output,
        own_bias_query,
        own_bias_value,
        own_bias_output,
        own_gain_first,
        own_shift_first,
        own_expand,
        own_bias_expand,
        own_shrink,
        own_bias_shrink,
        own_gain_second,
        own_shift_second,
    )


def solution(mesh):
    split = P("dp")
    wide = P("dp", None)
    return jax.shard_map(
        functools.partial(body, count=mesh.shape["dp"]),
        mesh=mesh,
        in_specs=(wide, split, split)
        + (wide,) * 4
        + (split,) * 5
        + (wide, split, wide, split, split, split, wide),
        out_specs=(wide,) * 6 + (split,) * 5 + (wide, split, wide, split, split, split),
        check_vma=False,
    )
```

time: 1200 us -> 431 us (0.36)
  waiting for transfers between devices: 703 us -> 124 us
  matrix products: 261 us -> 0 us
  Pallas kernels: 0 us -> 207 us
  blocking collectives: 83.1 us -> 0 us
  local copies, waits for them, and re-layouts: 89.1 us -> 28.8 us
  starting transfers between devices: 0.94 us -> 36.6 us
  other arithmetic: 39.2 us -> 14.2 us
    reduce_scatter x3 -> x0, waiting for transfers between devices: 387 us -> none  [the longest x1 142 us: body(): lax.psum_scatter(grad_w_shrink, 'dp', scatter_dimension=0, tiled=True)]
    dot_general x23 -> x0, matrix products: 243 us -> none  [the longest x1 49.6 us: ffn_forward(): jnp.dot(first_low, full_expand, preferred_element_type=jnp.float32)]
    pallas_call x0 -> x16, Pallas kernels: none -> 207 us  [the longest x1 48.4 us: ffn_fwd(): pl.pallas_call(ffn_fwd_kernel, grid_spec=pltpu.PrefetchScalarGridSpec(num...]
    all_gather x6 -> x1, waiting for transfers between devices: 166 us -> 0.01 us  [body(): whole = lambda v: lax.all_gather(v, 'dp', axis=0, tiled=True)]
    unnamed x15 -> x1, waiting for transfers between devices: 150 us -> 0.68 us
    ppermute x0 -> x34, waiting for transfers between devices: none -> 123 us  [exchange(): return lax.ppermute(value, 'dp', pairs)]
    unnamed x2 -> x0, blocking collectives: 83.1 us -> none
    ppermute x0 -> x34, starting transfers between devices: none -> 36.5 us  [exchange(): return lax.ppermute(value, 'dp', pairs)]
  transfers between devices with their start and end apart: 12 -> 35, of which waited for: 10 -> 16; matrix products, arithmetic and copies ran while one was open for 22% -> 6% of each run, Pallas kernels for 0% -> 25%
where the time goes in v1:
time: 431 us; the launch traced here: 425 us
  Pallas kernels  207 us (48%)
  waiting for transfers between devices  124 us (29%)
  starting transfers between devices  36.6 us (8%)
  local copies, waits for them, and re-layouts  28.8 us (7%)
  between operations  14.7 us (3%)
  other arithmetic  14.2 us (3%)
    ppermute x34, waiting for transfers between devices, exchange(): return lax.ppermute(value, 'dp', pairs)  123 us
    pallas_call x1, Pallas kernels, ffn_fwd(): pl.pallas_call(ffn_fwd_kernel, grid_spec=pltpu.PrefetchScalarGridSpec(num...  48.4 us
    pallas_call x6, Pallas kernels, grad_w(): pl.pallas_call(tn_kernel, grid=grid, in_specs=[pl.BlockSpec((R, bm), ia),...  46.4 us
    ppermute x34, starting transfers between devices, exchange(): return lax.ppermute(value, 'dp', pairs)  36.5 us
    pallas_call x1, Pallas kernels, ffn_bwd(): pl.pallas_call(ffn_bwd_kernel, grid=(S,), in_specs=[rb(D), rb(D), rb(FF),...  30.2 us
    pallas_call x1, Pallas kernels, attn_bwd(): pl.pallas_call(attn_bwd_kernel, grid_spec=pltpu.PrefetchScalarGridSpec(nu...  27 us
    pallas_call x1, Pallas kernels, attn_fwd(): pl.pallas_call(attn_fwd_kernel, grid_spec=pltpu.PrefetchScalarGridSpec(nu...  21.9 us
    unnamed x35, local copies, waits for them, and re-layouts  15.6 us
  transfers between devices with their start and end apart: 35, of which 16 were waited for; matrix products, arithmetic and copies ran while one was open for 6% of the time, Pallas kernels for 25%

profile of v1, /device:TPU:0, one launch (start us, length us, event | category | flops | bytes accessed | tf_op | source)
XLA Modules:
  0.0 424.6 jit_solution(6427617430034653577)
XLA Ops:
  7.9 6.1 %concatenate.35 = bf16[288]{0:T(512)(128)(2,1)S(1)} concatenate(bf16[24]{0:T(256)(128)(2,1)} %param.28, bf16[24]{0:T(256)(128)(2,1)} %param.29, bf16[24]{0:T(256)(128)(2,1)} %param.30, bf16[24]{0:T(256)(128)(2,1)} %param.34, bf16[24]{0:T(256)(128)(2,1)} %param.35, bf16[24]{0:T(256)(128)(2,1)} %param.36, bf16[24]{0:T(256)(128)(2,1)} %param.26, bf16[24]{0:T(256)(128)(2,1)} %param.27, ...), dimensions={0} | concatenate | bytes 1152 | tf_op jit(solution)/shard_map/concatenate | solution.py:400
  14.9 3.1 collective-permute-start
  17.9 2.6 collective-permute-start.1
  21.3 0.9 constant_dynamic-update-slice_fusion.5
  22.2 1.0 collective-permute-start.8
  23.2 3.5 collective-permute-start.9
  27.6 4.7 %collective-permute-done.1 = bf16[80,768]{1,0:T(8,128)(2,1)S(1)} collective-permute-done((bf16[80,768]{1,0:T(8,128)(2,1)S(1)}, bf16[80,768]{1,0:T(8,128)(2,1)S(1)}, u32[]{:S(2)}, u32[]{:S(2)}) %collective-permute-start.1) | collective-permute-done | bytes 122912 | tf_op jit(solution)/shard_map/ppermute | solution.py:265
  32.4 1.5 collective-permute-start.3
  33.9 1.5 collective-permute-done.8
  35.4 12.6 %collective-permute-done.9 = bf16[120,768]{1,0:T(8,128)(2,1)S(1)} collective-permute-done((bf16[120,768]{1,0:T(8,128)(2,1)S(1)}, bf16[120,768]{1,0:T(8,128)(2,1)S(1)}, u32[]{:S(2)}, u32[]{:S(2)}) %collective-permute-start.9) | collective-permute-done | bytes 184352 | tf_op jit(solution)/shard_map/ppermute | solution.py:265
  48.1 1.6 collective-permute-start.11
  49.7 15.4 %collective-permute-done.11.refs_1_ = bf16[4,120,768]{2,1,0:T(8,128)(2,1)S(1)} collective-permute-done((bf16[4,120,768]{2,1,0:T(8,128)(2,1)S(1)}, bf16[4,120,768]{2,1,0:T(8,128)(2,1)S(1)}, u32[]{:S(2)}, u32[]{:S(2)}) %collective-permute-start.11) | collective-permute-done | bytes 737312 | tf_op jit(solution)/shard_map/ppermute | solution.py:265
  65.1 1.5 collective-permute-start.12
  67.3 36.2 %collective-permute-done.4.refs_2_ = bf16[8,80,768]{2,1,0:T(8,128)(2,1)S(1)} collective-permute-done((bf16[8,80,768]{2,1,0:T(8,128)(2,1)S(1)}, bf16[8,80,768]{2,1,0:T(8,128)(2,1)S(1)}, u32[]{:S(2)}, u32[]{:S(2)}) %collective-permute-start.4) | collective-permute-done | bytes 983072 | tf_op jit(solution)/shard_map/ppermute | solution.py:265
  104.5 4.4 %collective-permute-done.5.refs_3_ = bf16[4,80,768]{2,1,0:T(8,128)(2,1)} collective-permute-done((bf16[4,80,768]{2,1,0:T(8,128)(2,1)S(1)}, bf16[4,80,768]{2,1,0:T(8,128)(2,1)}, u32[]{:S(2)}, u32[]{:S(2)}) %collective-permute-start.5) | collective-permute-done | bytes 491552 | tf_op jit(solution)/shard_map/ppermute | solution.py:265
  109.7 4.1 unpack_qkv.1
  113.8 1.0 copy-done.7
  114.8 1.0 copy-done.8
  115.9 1.0 copy-done.9
  118.6 21.9 %attn_fwd.1 = (bf16[1536,768]{1,0:T(8,128)(2,1)}, bf16[1536,768]{1,0:T(8,128)(2,1)}, bf16[1536,768]{1,0:T(8,128)(2,1)}, bf16[1536,768]{1,0:T(8,128)(2,1)}, bf16[1536,128]{1,0:T(8,128)(2,1)}) custom-call(s32[4]{0:T(128)} %len_ref.3, bf16[1536,768]{1,0:T(8,128)(2,1)} %a_ref.5, bf16[768,768]{1,0:T(8,128)(2,1)} %bitcast.93, bf16[768,768]{1,0:T(8,128)(2,1)} %bitcast.95, ...), custom_call_target="tpu_custom_call" | custom-call | flops 8999999488 | bytes 20000000 | tf_op jit(solution)/shard_map/attn_fwd/pallas_call | solution.py:66
  140.5 3.9 unpack_shrink.1
  144.4 2.2 copy-done.6
  146.5 1.0 copy-done.10
  147.6 48.4 %ffn_fwd.1 = (f32[1536,768]{1,0:T(8,128)}, f32[1536,128]{1,0:T(8,128)}, bf16[1536,768]{1,0:T(8,128)(2,1)}, bf16[1536,3072]{1,0:T(8,128)(2,1)}, bf16[1536,3072]{1...) custom-call(s32[4]{0:T(128)} %bk_ref.1, ...), custom_call_target="tpu_custom_call" | custom-call | flops 16999999488 | bytes 60000000 | tf_op jit(solution)/shard_map/ffn_fwd/pallas_call | solution.py:188
  196.7 30.2 %ffn_bwd.1 = (bf16[1536,3072]{1,0:T(8,128)(2,1)}, f32[1536,768]{1,0:T(8,128)}, bf16[1536,768]{1,0:T(8,128)(2,1)}, bf16[1536,768]{1,0:T(8,128)(2,1)}, f32[8,768]{1,0:T(8,128)}, /*index=5*/f32[1,3072]{1,0:T(1,128)}) custom-call(bf16[1536,768]{1,0:T(8,128)(2,1)} %get-tuple-element.61.gs_ref.b_ref, f32[1536,768]{1,0:T(8,128)} %get-tuple-element.62.gh_ref, ...), custom_call_target="tpu_custom_call" | custom-call | flops 16999999488 | bytes 60000000 | tf_op jit(solution)/shard_map/ffn_bwd/pallas_call | solution.py:231
  226.9 5.8 %dw_output.1 = bf16[768,768]{1,0:T(8,128)(2,1)} custom-call(bf16[1536,768]{1,0:T(8,128)(2,1)} %get-tuple-element.57.c_ref.a_ref, bf16[1536,768]{1,0:T(8,128)(2,1)} %get-tuple-element.83.b_ref), custom_call_target="tpu_custom_call" | custom-call | flops 1811939328 | bytes 5898240 | tf_op jit(solution)/shard_map/dw_output/pallas_call | solution.py:247
  232.6 11.8 %dw_expand.1 = bf16[768,3072]{1,0:T(8,128)(2,1)} custom-call(bf16[1536,768]{1,0:T(8,128)(2,1)} %get-tuple-element.81.a_ref, bf16[1536,3072]{1,0:T(8,128)(2,1)} %get-tuple-element.82.b_ref), custom_call_target="tpu_custom_call" | custom-call | flops 7247757312 | bytes 16515072 | tf_op jit(solution)/shard_map/dw_expand/pallas_call | solution.py:247
  244.4 2.3 copy-done
  246.7 3.4 pack_expand.1
  250.4 27.0 %attn_bwd.1 = (bf16[1536,768]{1,0:T(8,128)(2,1)}, bf16[1536,768]{1,0:T(8,128)(2,1)}, bf16[1536,768]{1,0:T(8,128)(2,1)}, f32[8,768]{1,0:T(8,128)}) custom-call(s32[4]{0:T(128)} %len_ref.3, bf16[1536,768]{1,0:T(8,128)(2,1)} %get-tuple-element.67.q_ref, bf16[1536,768]{1,0:T(8,128)(2,1)} %get-tuple-element.68.k_ref, bf16[1536,768]{1,0:T(8,128)(2,1)} %get-tuple-element.69.v_ref, ...), custom_call_target="tpu_custom_call" | custom-call | flops 15000000512 | bytes 24000000 | tf_op jit(solution)/shard_map/attn_bwd/pallas_call | solution.py:122
  279.3 5.7 %dw_query.1 = bf16[768,768]{1,0:T(8,128)(2,1)} custom-call(bf16[1536,768]{1,0:T(8,128)(2,1)} %a_ref.5, bf16[1536,768]{1,0:T(8,128)(2,1)} %get-tuple-element.72.a_ref.b_ref), custom_call_target="tpu_custom_call" | custom-call | flops 1811939328 | bytes 5898240 | tf_op jit(solution)/shard_map/dw_query/pallas_call | solution.py:247
  285.0 5.7 %dw_key.1 = bf16[768,768]{1,0:T(8,128)(2,1)} custom-call(bf16[1536,768]{1,0:T(8,128)(2,1)} %a_ref.5, bf16[1536,768]{1,0:T(8,128)(2,1)} %get-tuple-element.73.b_ref), custom_call_target="tpu_custom_call" | custom-call | flops 1811939328 | bytes 5898240 | tf_op jit(solution)/shard_map/dw_key/pallas_call | solution.py:247
  290.8 5.8 %dw_value.1 = bf16[768,768]{1,0:T(8,128)(2,1)} custom-call(bf16[1536,768]{1,0:T(8,128)(2,1)} %a_ref.5, bf16[1536,768]{1,0:T(8,128)(2,1)} %get-tuple-element.74.c_ref.b_ref), custom_call_target="tpu_custom_call" | custom-call | flops 1811939328 | bytes 5898240 | tf_op jit(solution)/shard_map/dw_value/pallas_call | solution.py:247
  296.7 1.3 copy-done.2
  297.9 1.3 copy-done.3
  299.2 1.3 copy-done.4
  300.5 3.9 pack_qkv.1
  304.8 11.7 %dw_shrink.1 = bf16[3072,768]{1,0:T(8,128)(2,1)} custom-call(bf16[1536,3072]{1,0:T(8,128)(2,1)} %get-tuple-element.86.a_ref, bf16[1536,768]{1,0:T(8,128)(2,1)} %get-tuple-element.61.gs_ref.b_ref), custom_call_target="tpu_custom_call" | custom-call | flops 7247757312 | bytes 16515072 | tf_op jit(solution)/shard_map/dw_shrink/pallas_call | solution.py:247
  316.5 2.3 copy-done.1
  318.8 6.4 %pack_shrink.1 = (bf16[16,96,768]{2,1,0:T(8,128)(2,1)S(1)}, bf16[16,96,768]{2,1,0:T(8,128)(2,1)S(1)}) custom-call(s32[1]{0:T(128)} %bitcast.me_ref, bf16[32,96,768]{2,1,0:T(8,128)(2,1)S(1)} %bitcast.86), custom_call_target="tpu_custom_call" | custom-call | bytes 9437184 | tf_op jit(solution)/shard_map/pack_shrink/pallas_call | solution.py:362
  325.4 2.0 add_convert_fusion.5
  327.3 1.5 collective-permute-start.17
  328.8 0.9 collective-permute-done.28
  329.8 1.7 add_convert_fusion.3
  331.5 1.4 collective-permute-start.29
  332.9 3.6 add_convert_fusion.1
  337.1 4.4 %collective-permute-done.17 = bf16[8,80,768]{2,1,0:T(8,128)(2,1)S(1)} collective-permute-done((bf16[8,80,768]{2,1,0:T(8,128)(2,1)S(1)}, bf16[8,80,768]{2,1,0:T(8,128)(2,1)S(1)}, u32[]{:S(2)}, u32[]{:S(2)}) %collective-permute-start.17) | collective-permute-done | bytes 983072 | tf_op jit(solution)/shard_map/ppermute | solution.py:265
  341.8 11.2 %grad_in.1 = f32[1536,768]{1,0:T(8,128)} custom-call(f32[1536,768]{1,0:T(8,128)} %get-tuple-element.66.gr_ref, bf16[1536,768]{1,0:T(8,128)(2,1)} %get-tuple-element.72.a_ref.b_ref, bf16[1536,768]{1,0:T(8,128)(2,1)} %get-tuple-element.73.b_ref, bf16[1536,768]{1,0:T(8,128)(2,1)} %get-tuple-element.74.c_ref.b_ref, bf16[768,768]{1,0:T(8,128)(2,1)} %bitcast.94, ...), custom_call_target="tpu_custom_call" | custom-call | flops 5435817984 | bytes 20000000 | tf_op jit(solution)/shard_map/grad_in/pallas_call | solution.py:257
  353.1 2.9 collective-permute-done.18
  356.1 1.4 collective-permute-start.19
  357.5 2.7 collective-permute-start.20
  360.5 1.5 add_convert_fusion.9
  362.1 1.1 collective-permute-start.30
  363.1 5.8 %collective-permute-done.20 = bf16[80,768]{1,0:T(8,128)(2,1)S(1)} collective-permute-done((bf16[80,768]{1,0:T(8,128)(2,1)S(1)}, bf16[80,768]{1,0:T(8,128)(2,1)S(1)}, u32[]{:S(2)}, u32[]{:S(2)}) %collective-permute-start.20) | collective-permute-done | bytes 122912 | tf_op jit(solution)/shard_map/ppermute | solution.py:265
  369.0 12.5 %collective-permute-done.23 = bf16[8,120,768]{2,1,0:T(8,128)(2,1)S(1)} collective-permute-done((bf16[8,120,768]{2,1,0:T(8,128)(2,1)}, bf16[8,120,768]{2,1,0:T(8,128)(2,1)S(1)}, u32[]{:S(2)}, u32[]{:S(2)}) %collective-permute-start.23) | collective-permute-done | bytes 1474592 | tf_op jit(solution)/shard_map/ppermute | solution.py:265
  384.0 3.0 collective-permute-start.31
  387.0 1.2 collective-permute-start.32
  388.1 1.3 collective-permute-start.33
  389.4 4.0 collective-permute-done.24
  393.6 1.4 collective-permute-start.25
  395.0 2.7 collective-permute-start.26
  398.0 2.9 collective-permute-done.32
  401.7 1.9 collective-permute-done.25
  403.7 12.3 %collective-permute-done.26 = bf16[120,768]{1,0:T(8,128)(2,1)S(1)} collective-permute-done((bf16[120,768]{1,0:T(8,128)(2,1)S(1)}, bf16[120,768]{1,0:T(8,128)(2,1)S(1)}, u32[]{:S(2)}, u32[]{:S(2)}) %collective-permute-start.26) | collective-permute-done | bytes 184352 | tf_op jit(solution)/shard_map/ppermute | solution.py:265
  (104 shorter events, 17.9 us)
Async XLA Ops:
  7.2 140.4 %all-gather.2.cloned.1.call-start = ((), (), s32[]{:S(2)}) async-start(), calls=%async_computation | async-start | bytes 4866048 | tf_op jit(solution)/shard_map/all_gather | solution.py:427
  14.9 12.7 %collective-permute-start = (bf16[80,768]{1,0:T(8,128)(2,1)S(1)}, bf16[80,768]{1,0:T(8,128)(2,1)S(1)}, u32[]{:S(2)}, u32[]{:S(2)}) collective-permute-start(bf16[80,768]{1,0:T(8,128)(2,1)S(1)} %get-tuple-element.127), channel_id=1, source_target_pairs={{0,8},{1,9},{2,10},{3,11},{4,12},{5,13},{6,14},{7,15},{8,0},{9,1},... | collective-permute-start | bytes 368648 | tf_op jit(solution)/shard_map/ppermute | solution.py:265
  17.9 14.3 %collective-permute-start.1 = (bf16[80,768]{1,0:T(8,128)(2,1)S(1)}, bf16[80,768]{1,0:T(8,128)(2,1)S(1)}, u32[]{:S(2)}, u32[]{:S(2)}) collective-permute-start(bf16[80,768]{1,0:T(8,128)(2,1)S(1)} %get-tuple-element.127), channel_id=1, source_target_pairs={{0,16},{1,17},{2,18},{3,19},{4,20},{5,21},{6,22},{7,23},{8,24},{9,... | collective-permute-start | bytes 368648 | tf_op jit(solution)/shard_map/ppermute | solution.py:265
  20.5 11.8 %collective-permute-start.2 = (bf16[80,768]{1,0:T(8,128)(2,1)S(1)}, bf16[80,768]{1,0:T(8,128)(2,1)S(1)}, u32[]{:S(2)}, u32[]{:S(2)}) collective-permute-start(bf16[80,768]{1,0:T(8,128)(2,1)S(1)} %get-tuple-element.127), channel_id=1, source_target_pairs={{0,24},{1,25},{2,26},{3,27},{4,28},{5,29},{6,30},{7,31},{8,16},{9,... | collective-permute-start | bytes 368648 | tf_op jit(solution)/shard_map/ppermute | solution.py:265
  22.2 13.1 %collective-permute-start.8 = (bf16[120,768]{1,0:T(8,128)(2,1)S(1)}, bf16[120,768]{1,0:T(8,128)(2,1)S(1)}, u32[]{:S(2)}, u32[]{:S(2)}) collective-permute-start(bf16[120,768]{1,0:T(8,128)(2,1)S(1)} %constant_dynamic-update-slice_fusion.5), channel_id=1, source_target_pairs={{0,8},{1,9},{2,10},{3,11},{4,12},{5,13},{6,14},{7,15},{8,0},{9,1},... | collective-permute-start | bytes 552968 | tf_op jit(solution)/shard_map/ppermute | solution.py:265
  23.2 24.8 %collective-permute-start.9 = (bf16[120,768]{1,0:T(8,128)(2,1)S(1)}, bf16[120,768]{1,0:T(8,128)(2,1)S(1)}, u32[]{:S(2)}, u32[]{:S(2)}) collective-permute-start(bf16[120,768]{1,0:T(8,128)(2,1)S(1)} %constant_dynamic-update-slice_fusion.5), channel_id=1, source_target_pairs={{0,16},{1,17},{2,18},{3,19},{4,20},{5,21},{6,22},{7,23},{8,24},{9,... | collective-permute-start | bytes 552968 | tf_op jit(solution)/shard_map/ppermute | solution.py:265
  27.5 20.4 %collective-permute-start.10 = (bf16[120,768]{1,0:T(8,128)(2,1)S(1)}, bf16[120,768]{1,0:T(8,128)(2,1)S(1)}, u32[]{:S(2)}, u32[]{:S(2)}) collective-permute-start(bf16[120,768]{1,0:T(8,128)(2,1)S(1)} %constant_dynamic-update-slice_fusion.5), channel_id=1, source_target_pairs={{0,24},{1,25},{2,26},{3,27},{4,28},{5,29},{6,30},{7,31},{8,16},{9,... | collective-permute-start | bytes 552968 | tf_op jit(solution)/shard_map/ppermute | solution.py:265
  32.4 34.3 %collective-permute-start.3 = (bf16[4,80,768]{2,1,0:T(8,128)(2,1)S(1)}, bf16[4,80,768]{2,1,0:T(8,128)(2,1)S(1)}, u32[]{:S(2)}, u32[]{:S(2)}) collective-permute-start(bf16[4,80,768]{2,1,0:T(8,128)(2,1)S(1)} %pad_maximum_fusion.1.refs_0_), channel_id=1, source_target_pairs={{0,2},{1,5},{2,0},{3,7},{4,6},{5,1},{6,4},{7,3},{8,10},{9,13},{10,... | collective-permute-start | bytes 1474568 | tf_op jit(solution)/shard_map/ppermute | solution.py:265
  48.1 17.0 %collective-permute-start.11 = (bf16[4,120,768]{2,1,0:T(8,128)(2,1)S(1)}, bf16[4,120,768]{2,1,0:T(8,128)(2,1)S(1)}, u32[]{:S(2)}, u32[]{:S(2)}) collective-permute-start(bf16[4,120,768]{2,1,0:T(8,128)(2,1)S(1)} %pad_maximum_fusion.refs_0_), channel_id=1, source_target_pairs={{0,2},{1,5},{2,0},{3,7},{4,6},{5,1},{6,4},{7,3},{8,10},{9,13},{10,... | collective-permute-start | bytes 2211848 | tf_op jit(solution)/shard_map/ppermute | solution.py:265
  65.1 38.4 %collective-permute-start.12 = (bf16[8,120,768]{2,1,0:T(8,128)(2,1)S(1)}, bf16[8,120,768]{2,1,0:T(8,128)(2,1)}, u32[]{:S(2)}, u32[]{:S(2)}) collective-permute-start(bf16[8,120,768]{2,1,0:T(8,128)(2,1)S(1)} %constant_dynamic-update-slice_fusion.7), channel_id=1, source_target_pairs={{0,4},{1,3},{2,6},{3,1},{4,0},{5,7},{6,2},{7,5},{8,12},{9,11},{10,... | collective-permute-start | bytes 4423688 | tf_op jit(solution)/shard_map/ppermute | solution.py:265
  66.7 36.8 %collective-permute-start.4 = (bf16[8,80,768]{2,1,0:T(8,128)(2,1)S(1)}, bf16[8,80,768]{2,1,0:T(8,128)(2,1)S(1)}, u32[]{:S(2)}, u32[]{:S(2)}) collective-permute-start(bf16[8,80,768]{2,1,0:T(8,128)(2,1)S(1)} %constant_dynamic-update-slice_fusion), channel_id=1, source_target_pairs={{0,4},{1,3},{2,6},{3,1},{4,0},{5,7},{6,2},{7,5},{8,12},{9,11},{10,... | collective-permute-start | bytes 2949128 | tf_op jit(solution)/shard_map/ppermute | solution.py:265
  103.5 6.2 %collective-permute-start.7 = (bf16[8,80,768]{2,1,0:T(8,128)(2,1)S(1)}, bf16[8,80,768]{2,1,0:T(8,128)(2,1)}, u32[]{:S(2)}, u32[]{:S(2)}) collective-permute-start(bf16[8,80,768]{2,1,0:T(8,128)(2,1)S(1)} %collective-permute-done.4.refs_2_), channel_id=1, source_target_pairs={{0,1},{1,0},{2,3},{3,2},{4,5},{5,4},{6,7},{7,6},{8,9},{9,8},{10,11... | collective-permute-start | bytes 2949128 | tf_op jit(solution)/shard_map/ppermute | solution.py:265
  103.5 36.9 %collective-permute-start.15 = (bf16[8,120,768]{2,1,0:T(8,128)(2,1)}, bf16[8,120,768]{2,1,0:T(8,128)(2,1)}, u32[]{:S(2)}, u32[]{:S(2)}) collective-permute-start(bf16[8,120,768]{2,1,0:T(8,128)(2,1)} %collective-permute-done.12.refs_2_), channel_id=1, source_target_pairs={{0,1},{1,0},{2,3},{3,2},{4,5},{5,4},{6,7},{7,6},{8,9},{9,8},{10,11... | collective-permute-start | bytes 4423688 | tf_op jit(solution)/shard_map/ppermute | solution.py:265
  104.0 4.9 %collective-permute-start.5 = (bf16[4,80,768]{2,1,0:T(8,128)(2,1)S(1)}, bf16[4,80,768]{2,1,0:T(8,128)(2,1)}, u32[]{:S(2)}, u32[]{:S(2)}) collective-permute-start(bf16[4,80,768]{2,1,0:T(8,128)(2,1)S(1)} %pad_maximum_fusion.1.refs_0_), channel_id=1, source_target_pairs={{0,1},{1,0},{2,3},{3,2},{4,5},{5,4},{6,7},{7,6},{8,9},{9,8},{10,11... | collective-permute-start | bytes 1474568 | tf_op jit(solution)/shard_map/ppermute | solution.py:265
  104.0 5.7 %collective-permute-start.6 = (bf16[4,80,768]{2,1,0:T(8,128)(2,1)S(1)}, bf16[4,80,768]{2,1,0:T(8,128)(2,1)}, u32[]{:S(2)}, u32[]{:S(2)}) collective-permute-start(bf16[4,80,768]{2,1,0:T(8,128)(2,1)S(1)} %collective-permute-done.3.refs_1_), channel_id=1, source_target_pairs={{0,1},{1,0},{2,3},{3,2},{4,5},{5,4},{6,7},{7,6},{8,9},{9,8},{10,11... | collective-permute-start | bytes 1474568 | tf_op jit(solution)/shard_map/ppermute | solution.py:265
  104.5 35.9 %collective-permute-start.13 = (bf16[4,120,768]{2,1,0:T(8,128)(2,1)S(1)}, bf16[4,120,768]{2,1,0:T(8,128)(2,1)}, u32[]{:S(2)}, u32[]{:S(2)}) collective-permute-start(bf16[4,120,768]{2,1,0:T(8,128)(2,1)S(1)} %pad_maximum_fusion.refs_0_), channel_id=1, source_target_pairs={{0,1},{1,0},{2,3},{3,2},{4,5},{5,4},{6,7},{7,6},{8,9},{9,8},{10,11... | collective-permute-start | bytes 2211848 | tf_op jit(solution)/shard_map/ppermute | solution.py:265
  108.9 31.5 %collective-permute-start.14 = (bf16[4,120,768]{2,1,0:T(8,128)(2,1)S(1)}, bf16[4,120,768]{2,1,0:T(8,128)(2,1)}, u32[]{:S(2)}, u32[]{:S(2)}) collective-permute-start(bf16[4,120,768]{2,1,0:T(8,128)(2,1)S(1)} %collective-permute-done.11.refs_1_), channel_id=1, source_target_pairs={{0,1},{1,0},{2,3},{3,2},{4,5},{5,4},{6,7},{7,6},{8,9},{9,8},{10,11... | collective-permute-start | bytes 2211848 | tf_op jit(solution)/shard_map/ppermute | solution.py:265
  113.8 1.0 copy-start.7
  114.8 1.0 copy-start.8
  115.9 1.0 copy-start.9
  144.4 2.2 copy-start.6
  146.5 1.0 copy-start.10
  196.7 30.2 %copy-start.11 = (bf16[8,768]{1,0:T(8,128)(2,1)}, bf16[8,768]{1,0:T(8,128)(2,1)S(1)}, u32[]{:S(2)}) copy-start(bf16[8,768]{1,0:T(8,128)(2,1)S(1)} %convert.26) | copy-start | bytes 36868
  232.6 11.8 %copy-start.5 = (bf16[768,768]{1,0:T(8,128)(2,1)S(1)}, bf16[768,768]{1,0:T(8,128)(2,1)}, u32[]{:S(2)}) copy-start(bf16[768,768]{1,0:T(8,128)(2,1)} %dw_output.1) | copy-start | bytes 3538948
  244.4 2.3 copy-start
  250.2 82.7 %collective-permute-start.22 = (bf16[16,120,768]{2,1,0:T(8,128)(2,1)}, bf16[16,120,768]{2,1,0:T(8,128)(2,1)}, u32[]{:S(2)}, u32[]{:S(2)}) collective-permute-start(bf16[16,120,768]{2,1,0:T(8,128)(2,1)} %get-tuple-element.85), channel_id=1, source_target_pairs={{0,1},{1,0},{2,3},{3,2},{4,5},{5,4},{6,7},{7,6},{8,9},{9,8},{10,11... | collective-permute-start | bytes 8847368 | tf_op jit(solution)/shard_map/ppermute | solution.py:265
  250.4 28.5 %slice-start = ((bf16[8,768]{1,0:T(8,128)(2,1)}), bf16[2,768]{1,0:T(2,128)(2,1)S(1)}, s32[]{:S(2)}) async-start(bf16[8,768]{1,0:T(8,128)(2,1)} %copy-done.11), calls=%async_computation.1 | async-start | bytes 6144 | tf_op jit(solution)/shard_map/slice | solution.py:510
  250.4 28.8 %copy-start.12 = (f32[1,3072]{1,0:T(1,128)S(1)}, f32[1,3072]{1,0:T(1,128)}, u32[]{:S(2)}) copy-start(f32[1,3072]{1,0:T(1,128)} %get-tuple-element.78) | copy-start | bytes 36868
  296.7 1.3 copy-start.2
  297.9 1.3 copy-start.3
  299.2 1.3 copy-start.4
  304.4 21.0 %collective-permute-start.16 = (bf16[16,80,768]{2,1,0:T(8,128)(2,1)}, bf16[16,80,768]{2,1,0:T(8,128)(2,1)}, u32[]{:S(2)}, u32[]{:S(2)}) collective-permute-start(bf16[16,80,768]{2,1,0:T(8,128)(2,1)} %get-tuple-element.80), channel_id=1, source_target_pairs={{0,1},{1,0},{2,3},{3,2},{4,5},{5,4},{6,7},{7,6},{8,9},{9,8},{10,11... | collective-permute-start | bytes 5898248 | tf_op jit(solution)/shard_map/ppermute | solution.py:265
  316.5 2.3 copy-start.1
  325.2 4.6 %collective-permute-start.28 = (bf16[16,96,768]{2,1,0:T(8,128)(2,1)S(1)}, bf16[16,96,768]{2,1,0:T(8,128)(2,1)S(1)}, u32[]{:S(2)}, u32[]{:S(2)}) collective-permute-start(bf16[16,96,768]{2,1,0:T(8,128)(2,1)S(1)} %get-tuple-element.88), channel_id=1, source_target_pairs={{0,1},{1,0},{2,3},{3,2},{4,5},{5,4},{6,7},{7,6},{8,9},{9,8},{10,11... | collective-permute-start | bytes 7077896 | tf_op jit(solution)/shard_map/ppermute | solution.py:265
  327.3 14.2 %collective-permute-start.17 = (bf16[8,80,768]{2,1,0:T(8,128)(2,1)S(1)}, bf16[8,80,768]{2,1,0:T(8,128)(2,1)S(1)}, u32[]{:S(2)}, u32[]{:S(2)}) collective-permute-start(bf16[8,80,768]{2,1,0:T(8,128)(2,1)S(1)} %get-tuple-element.94), channel_id=1, source_target_pairs={{0,4},{1,3},{2,6},{3,1},{4,0},{5,7},{6,2},{7,5},{8,12},{9,11},{10,... | collective-permute-start | bytes 2949128 | tf_op jit(solution)/shard_map/ppermute | solution.py:265
  331.5 29.1 %collective-permute-start.29 = (bf16[8,96,768]{2,1,0:T(8,128)(2,1)}, bf16[8,96,768]{2,1,0:T(8,128)(2,1)}, u32[]{:S(2)}, u32[]{:S(2)}) collective-permute-start(bf16[8,96,768]{2,1,0:T(8,128)(2,1)} %get-tuple-element.92), channel_id=1, source_target_pairs={{0,4},{1,3},{2,6},{3,1},{4,0},{5,7},{6,2},{7,5},{8,12},{9,11},{10,... | collective-permute-start | bytes 3538952 | tf_op jit(solution)/shard_map/ppermute | solution.py:265
  336.5 45.0 %collective-permute-start.23 = (bf16[8,120,768]{2,1,0:T(8,128)(2,1)}, bf16[8,120,768]{2,1,0:T(8,128)(2,1)S(1)}, u32[]{:S(2)}, u32[]{:S(2)}) collective-permute-start(bf16[8,120,768]{2,1,0:T(8,128)(2,1)} %get-tuple-element.90), channel_id=1, source_target_pairs={{0,4},{1,3},{2,6},{3,1},{4,0},{5,7},{6,2},{7,5},{8,12},{9,11},{10,... | collective-permute-start | bytes 4423688 | tf_op jit(solution)/shard_map/ppermute | solution.py:265
  341.8 14.2 %collective-permute-start.18 = (bf16[4,80,768]{2,1,0:T(8,128)(2,1)S(1)}, bf16[4,80,768]{2,1,0:T(8,128)(2,1)S(1)}, u32[]{:S(2)}, u32[]{:S(2)}) collective-permute-start(bf16[4,80,768]{2,1,0:T(8,128)(2,1)S(1)} %get-tuple-element.100), channel_id=1, source_target_pairs={{0,2},{1,5},{2,0},{3,7},{4,6},{5,1},{6,4},{7,3},{8,10},{9,13},{10,... | collective-permute-start | bytes 1474568 | tf_op jit(solution)/shard_map/ppermute | solution.py:265
  356.1 7.1 %collective-permute-start.19 = (bf16[80,768]{1,0:T(8,128)(2,1)S(1)}, bf16[80,768]{1,0:T(8,128)(2,1)S(1)}, u32[]{:S(2)}, u32[]{:S(2)}) collective-permute-start(bf16[80,768]{1,0:T(8,128)(2,1)S(1)} %get-tuple-element.107), channel_id=1, source_target_pairs={{0,8},{1,9},{2,10},{3,11},{4,12},{5,13},{6,14},{7,15},{8,0},{9,1},... | collective-permute-start | bytes 368648 | tf_op jit(solution)/shard_map/ppermute | solution.py:265
  357.5 11.4 %collective-permute-start.20 = (bf16[80,768]{1,0:T(8,128)(2,1)S(1)}, bf16[80,768]{1,0:T(8,128)(2,1)S(1)}, u32[]{:S(2)}, u32[]{:S(2)}) collective-permute-start(bf16[80,768]{1,0:T(8,128)(2,1)S(1)} %get-tuple-element.109), channel_id=1, source_target_pairs={{0,16},{1,17},{2,18},{3,19},{4,20},{5,21},{6,22},{7,23},{8,24},{9,... | collective-permute-start | bytes 368648 | tf_op jit(solution)/shard_map/ppermute | solution.py:265
  360.2 8.7 %collective-permute-start.21 = (bf16[80,768]{1,0:T(8,128)(2,1)S(1)}, bf16[80,768]{1,0:T(8,128)(2,1)S(1)}, u32[]{:S(2)}, u32[]{:S(2)}) collective-permute-start(bf16[80,768]{1,0:T(8,128)(2,1)S(1)} %get-tuple-element.108), channel_id=1, source_target_pairs={{0,24},{1,25},{2,26},{3,27},{4,28},{5,29},{6,30},{7,31},{8,16},{9,... | collective-permute-start | bytes 368648 | tf_op jit(solution)/shard_map/ppermute | solution.py:265
  362.1 21.8 %collective-permute-start.30 = (bf16[4,96,768]{2,1,0:T(8,128)(2,1)S(1)}, bf16[4,96,768]{2,1,0:T(8,128)(2,1)S(1)}, u32[]{:S(2)}, u32[]{:S(2)}) collective-permute-start(bf16[4,96,768]{2,1,0:T(8,128)(2,1)S(1)} %get-tuple-element.98), channel_id=1, source_target_pairs={{0,2},{1,5},{2,0},{3,7},{4,6},{5,1},{6,4},{7,3},{8,10},{9,13},{10,... | collective-permute-start | bytes 1769480 | tf_op jit(solution)/shard_map/ppermute | solution.py:265
  381.9 11.5 %collective-permute-start.24 = (bf16[4,120,768]{2,1,0:T(8,128)(2,1)S(1)}, bf16[4,120,768]{2,1,0:T(8,128)(2,1)S(1)}, u32[]{:S(2)}, u32[]{:S(2)}) collective-permute-start(bf16[4,120,768]{2,1,0:T(8,128)(2,1)S(1)} %get-tuple-element.96), channel_id=1, source_target_pairs={{0,2},{1,5},{2,0},{3,7},{4,6},{5,1},{6,4},{7,3},{8,10},{9,13},{10,... | collective-permute-start | bytes 2211848 | tf_op jit(solution)/shard_map/ppermute | solution.py:265
  384.0 13.8 %collective-permute-start.31 = (bf16[96,768]{1,0:T(8,128)(2,1)S(1)}, bf16[96,768]{1,0:T(8,128)(2,1)S(1)}, u32[]{:S(2)}, u32[]{:S(2)}) collective-permute-start(bf16[96,768]{1,0:T(8,128)(2,1)S(1)} %get-tuple-element.104), channel_id=1, source_target_pairs={{0,8},{1,9},{2,10},{3,11},{4,12},{5,13},{6,14},{7,15},{8,0},{9,1},... | collective-permute-start | bytes 442376 | tf_op jit(solution)/shard_map/ppermute | solution.py:265
  387.0 14.0 %collective-permute-start.32 = (bf16[96,768]{1,0:T(8,128)(2,1)S(1)}, bf16[96,768]{1,0:T(8,128)(2,1)S(1)}, u32[]{:S(2)}, u32[]{:S(2)}) collective-permute-start(bf16[96,768]{1,0:T(8,128)(2,1)S(1)} %get-tuple-element.106), channel_id=1, source_target_pairs={{0,16},{1,17},{2,18},{3,19},{4,20},{5,21},{6,22},{7,23},{8,24},{9,... | collective-permute-start | bytes 442376 | tf_op jit(solution)/shard_map/ppermute | solution.py:265
  388.1 12.8 %collective-permute-start.33 = (bf16[96,768]{1,0:T(8,128)(2,1)S(1)}, bf16[96,768]{1,0:T(8,128)(2,1)S(1)}, u32[]{:S(2)}, u32[]{:S(2)}) collective-permute-start(bf16[96,768]{1,0:T(8,128)(2,1)S(1)} %get-tuple-element.105), channel_id=1, source_target_pairs={{0,24},{1,25},{2,26},{3,27},{4,28},{5,29},{6,30},{7,31},{8,16},{9,... | collective-permute-start | bytes 442376 | tf_op jit(solution)/shard_map/ppermute | solution.py:265
  393.6 10.1 %collective-permute-start.25 = (bf16[120,768]{1,0:T(8,128)(2,1)S(1)}, bf16[120,768]{1,0:T(8,128)(2,1)S(1)}, u32[]{:S(2)}, u32[]{:S(2)}) collective-permute-start(bf16[120,768]{1,0:T(8,128)(2,1)S(1)} %get-tuple-element.101), channel_id=1, source_target_pairs={{0,8},{1,9},{2,10},{3,11},{4,12},{5,13},{6,14},{7,15},{8,0},{9,1},... | collective-permute-start | bytes 552968 | tf_op jit(solution)/shard_map/ppermute | solution.py:265
  395.0 21.0 %collective-permute-start.26 = (bf16[120,768]{1,0:T(8,128)(2,1)S(1)}, bf16[120,768]{1,0:T(8,128)(2,1)S(1)}, u32[]{:S(2)}, u32[]{:S(2)}) collective-permute-start(bf16[120,768]{1,0:T(8,128)(2,1)S(1)} %get-tuple-element.103), channel_id=1, source_target_pairs={{0,16},{1,17},{2,18},{3,19},{4,20},{5,21},{6,22},{7,23},{8,24},{9,... | collective-permute-start | bytes 552968 | tf_op jit(solution)/shard_map/ppermute | solution.py:265
  397.7 18.2 %collective-permute-start.27 = (bf16[120,768]{1,0:T(8,128)(2,1)S(1)}, bf16[120,768]{1,0:T(8,128)(2,1)S(1)}, u32[]{:S(2)}, u32[]{:S(2)}) collective-permute-start(bf16[120,768]{1,0:T(8,128)(2,1)S(1)} %get-tuple-element.102), channel_id=1, source_target_pairs={{0,24},{1,25},{2,26},{3,27},{4,28},{5,29},{6,30},{7,31},{8,16},{9,... | collective-permute-start | bytes 552968 | tf_op jit(solution)/shard_map/ppermute | solution.py:265
Sparse Core Ops, SparseCore 0:
  10.9 81.7 all-gather.1
